TPU v7x, 32 devices: a whole 2x2x4 slice. The times are simulated.
32 devices in a mesh: dp: 4 (over y, x), ctx: 8 (over z, core).
Axes of the slice: x: 2, y: 2, z: 4, core: 2. Of those that a mesh axis runs over, the one named last changes fastest.
Arguments:
- tokens: bfloat16 [2, 4, 1024, 768], P(None, 'dp', 'ctx'), may hold values from -6 to 6
- lengths: int32 [2, 4], P(None, 'dp'), may hold values from 256 to 1024, as said below
- routes: int32 [2, 4, 1024, 2], P(None, 'dp', 'ctx'), may hold values from 0 to 3, all different within a row
- rel_table: int32 [1024], replicated, may hold values from 0 to 31
- rel_bias: float32 [32, 12], replicated, may hold values from -5 to 5
- cotangent: bfloat16 [2, 4, 1024, 768], P(None, 'dp', 'ctx'), may hold values from -6 to 6
- w_qkv: bfloat16 [768, 2304], P('dp'), may hold values from -0.21875 to 0.21875
- w_attn: bfloat16 [768, 768], P('dp'), may hold values from -2.5 to 2.5
- w_router: bfloat16 [768, 4], P('dp'), may hold values from -0.15625 to 0.15625
- gain_attn: bfloat16 [768], P('dp'), may hold values from 0.5 to 1.5
- gain_moe: bfloat16 [768], P('dp'), may hold values from 0.5 to 1.5
- w_expert_in: bfloat16 [4, 768, 3072], P(None, 'dp'), may hold values from -0.21875 to 0.21875
- w_expert_out: bfloat16 [4, 3072, 768], P(None, 'dp'), may hold values from -0.109375 to 0.109375
Outputs:
- output: bfloat16 [2, 4, 1024, 768], P(None, 'dp', 'ctx')
- d_tokens: bfloat16 [2, 4, 1024, 768], P(None, 'dp', 'ctx')
- d_w_qkv: float32 [768, 2304], P(('dp', 'ctx'))
- d_w_attn: float32 [768, 768], P(('dp', 'ctx'))
- d_w_router: float32 [768, 4], P(('dp', 'ctx'))
- d_gain_attn: float32 [768], P(('dp', 'ctx'))
- d_gain_moe: float32 [768], P(('dp', 'ctx'))
- d_w_expert_in: float32 [4, 768, 3072], P(None, ('dp', 'ctx'))
- d_w_expert_out: float32 [4, 3072, 768], P(None, ('dp', 'ctx'))
- d_rel_bias: float32 [384], P(('dp', 'ctx'))
Inputs may be any that keep to these rules, and one draw needn't show every extreme that they name: `lengths`: for each sequence index one of the 2 micro-batches has length 1024. `routes`: the two experts of a slot differ.
All inputs are finite; a program needn't handle non-finite values.
Results may differ from a plain program's by a relative error of at most 0.028.
Values may be sent and summed in bfloat16 or wider, within the bound.
A program may use at most 512 MiB of HBM per device.

v0:
```python
import math

import jax
import jax.numpy as jnp
from jax import lax
from jax.sharding import PartitionSpec as P

EPSILON = 1e-06
NEGATIVE = -1e30
HIGH = lax.Precision.HIGHEST
MARGIN = 512


def outer_dot(left, right):
    return lax.dot_general(
        left, right, (((0,), (0,)), ((), ())), preferred_element_type=jnp.float32
    )


def back_dot(left, right):
    return lax.dot_general(
        left, right, (((1,), (1,)), ((), ())), preferred_element_type=jnp.float32
    )


def plain_dot(left, right):
    return jnp.dot(left, right, preferred_element_type=jnp.float32)


def rms_scale(values):
    return lax.rsqrt(jnp.mean(values * values, axis=-1, keepdims=True) + EPSILON)


def gelu_slope(hidden):
    return (
        0.5 * (1.0 + jax.scipy.special.erf(hidden * 0.7071067811865476))
        + hidden * jnp.exp(-0.5 * hidden * hidden) * 0.3989422804014327
    )


def norm_back(grad, scaled, gain, factor):
    inner = grad * gain
    return (
        factor * (inner - scaled * jnp.mean(inner * scaled, axis=-1, keepdims=True)),
        jnp.sum(grad * scaled, axis=0),
    )


def pad_bias(dist_bias):
    span = dist_bias.shape[1]
    return jnp.pad(dist_bias, ((0, 0), (span + MARGIN, span + MARGIN)))


def bias_block(padded, span, first_query, first_key, queries, keys_count):
    heads = padded.shape[0]
    extent = queries + keys_count - 1
    base = first_query - first_key - (keys_count - 1) + span + MARGIN
    window = lax.dynamic_slice_in_dim(padded, base, extent, 1)
    turned = window[:, ::-1]
    rolled = jnp.concatenate([turned[:, queries - 1 :], turned[:, : queries - 1]], axis=1)
    flat = jnp.tile(rolled, (1, queries))[:, : queries * (extent - 1)]
    return flat.reshape(heads, queries, extent - 1)[:, :, :keys_count]


def bias_grad(grad, queries, keys_count):
    heads = grad.shape[0]
    extent = queries + keys_count - 1
    flat = jnp.pad(grad, ((0, 0), (0, 0), (0, extent - 1 - keys_count))).reshape(
        heads, queries * (extent - 1)
    )
    folded = jnp.sum(jnp.pad(flat, ((0, 0), (0, queries))).reshape(heads, queries, extent), axis=1)
    cut = extent - (queries - 1)
    turned = jnp.concatenate([folded[:, cut:], folded[:, :cut]], axis=1)
    return turned[:, ::-1]


def attend_forward(
    query_low, query_pos, length, padded, span, scale, carry, key_piece, value_piece
):
    count = key_piece.shape[0]
    width = math.gcd(count, 512)
    blocks = count // width
    heads, head_size = (query_low.shape[1], query_low.shape[2])
    queries = query_low.shape[0]
    key_blocks = key_piece.reshape(blocks, width, heads, head_size)
    value_blocks = value_piece.reshape(blocks, width, heads, head_size)

    def step(state, item):
        index, key_block, value_block = item
        first_key = index * width
        key_pos = first_key + jnp.arange(width, dtype=jnp.int32)
        allowed = (key_pos[None, :] <= query_pos[:, None]) & (key_pos[None, :] < length)

        def work(inner):
            top, total, accum = inner
            scores = (
                jnp.einsum("qhd,khd->hqk", query_low, key_block, preferred_element_type=jnp.float32)
                * scale
            )
            scores = scores + bias_block(padded, span, query_pos[0], first_key, queries, width)
            scores = jnp.where(allowed[None], scores, NEGATIVE)
            new_top = jnp.maximum(top, jnp.max(scores, axis=-1))
            weights = jnp.where(allowed[None], jnp.exp(scores - new_top[:, :, None]), 0.0)
            decay = jnp.exp(top - new_top)
            total = total * decay + jnp.sum(weights, axis=-1)
            accum = accum * decay.T[:, :, None] + jnp.einsum(
                "hqk,khd->qhd",
                weights.astype(jnp.bfloat16),
                value_block,
                preferred_element_type=jnp.float32,
            )
            return (new_top, total, accum)

        return (lax.cond(jnp.any(allowed), work, lambda inner: inner, state), None)

    state, ignored = lax.scan(
        step, carry, (jnp.arange(blocks, dtype=jnp.int32), key_blocks, value_blocks)
    )
    return state


def attend_backward(
    query_low,
    grad_low,
    out_float,
    query_pos,
    length,
    padded,
    span,
    lse,
    scale,
    key_whole,
    value_whole,
):
    width_all = key_whole.shape[1]
    heads, head_size = (query_low.shape[1], query_low.shape[2])
    slots = query_low.shape[0]
    width = math.gcd(span, 512)
    blocks = span // width
    extent = slots + width - 1
    delta = jnp.sum(grad_low.astype(jnp.float32) * out_float, axis=-1).T

    def step(state, item):
        index, key_block, value_block = item
        first_key = index * width
        key_pos = first_key + jnp.arange(width, dtype=jnp.int32)
        allowed = (key_pos[None, :] <= query_pos[:, None]) & (key_pos[None, :] < length)

        def work(inner):
            d_query, d_dist = inner
            scores = (
                jnp.einsum("qhd,khd->hqk", query_low, key_block, preferred_element_type=jnp.float32)
                * scale
            )
            scores = scores + bias_block(padded, span, query_pos[0], first_key, slots, width)
            probs = jnp.where(allowed[None], jnp.exp(scores - lse[:, :, None]), 0.0)
            d_probs = jnp.einsum(
                "qhd,khd->hqk", grad_low, value_block, preferred_element_type=jnp.float32
            )
            d_scores = (probs * (d_probs - delta[:, :, None])).astype(jnp.bfloat16)
            d_query = (
                d_query
                + jnp.einsum(
                    "hqk,khd->qhd", d_scores, key_block, preferred_element_type=jnp.float32
                )
                * scale
            )
            d_keys = (
                jnp.einsum("hqk,qhd->khd", d_scores, query_low, preferred_element_type=jnp.float32)
                * scale
            )
            d_values = jnp.einsum(
                "hqk,qhd->khd",
                probs.astype(jnp.bfloat16),
                grad_low,
                preferred_element_type=jnp.float32,
            )
            base = query_pos[0] - first_key - (width - 1) + span + MARGIN
            window = lax.dynamic_slice_in_dim(d_dist, base, extent, 1)
            window = window + bias_grad(d_scores.astype(jnp.float32), slots, width)
            d_dist = lax.dynamic_update_slice_in_dim(d_dist, window, base, 1)
            joined = jnp.concatenate(
                [d_keys.reshape(width, width_all), d_values.reshape(width, width_all)], axis=1
            )
            return ((d_query, d_dist), joined)

        def skip(inner):
            return (inner, jnp.zeros((width, 2 * width_all), jnp.float32))

        return lax.cond(jnp.any(allowed), work, skip, state)

    init = (jnp.zeros((slots, heads, head_size), jnp.float32), jnp.zeros(padded.shape, jnp.float32))
    final, pieces = lax.scan(
        step,
        init,
        (
            jnp.arange(blocks, dtype=jnp.int32),
            key_whole.reshape(blocks, width, heads, head_size),
            value_whole.reshape(blocks, width, heads, head_size),
        ),
    )
    d_dist = final[1][:, span + MARGIN : 2 * span + MARGIN]
    return (final[0], d_dist, pieces.reshape(span, 2 * width_all))


def local(
    tokens,
    lengths,
    routes,
    rel_table,
    rel_bias,
    cotangent,
    w_qkv,
    w_attn,
    w_router,
    gain_attn,
    gain_moe,
    w_expert_in,
    w_expert_out,
):
    slots = tokens.shape[2]
    width = tokens.shape[3]
    span = rel_table.shape[0]
    heads = rel_bias.shape[1]
    head_size = width // heads
    experts = w_expert_in.shape[0]
    micro_count = tokens.shape[0]
    scale = head_size ** (-0.5)
    query_pos = lax.axis_index("ctx") * slots + jnp.arange(slots, dtype=jnp.int32)
    buckets = (
        rel_table[:, None] == jnp.arange(rel_bias.shape[0], dtype=jnp.int32)[None, :]
    ).astype(jnp.float32)
    dist_bias = jnp.dot(rel_bias.T, buckets.T, precision=HIGH)
    padded = pad_bias(dist_bias)
    held = (
        lax.all_gather(w_qkv, "dp", axis=0, tiled=True),
        lax.all_gather(w_attn, "dp", axis=0, tiled=True),
        lax.all_gather(w_router, "dp", axis=0, tiled=True),
        lax.all_gather(gain_attn, "dp", axis=0, tiled=True),
        lax.all_gather(gain_moe, "dp", axis=0, tiled=True),
        lax.all_gather(w_expert_in, "dp", axis=1, tiled=True),
        lax.all_gather(w_expert_out, "dp", axis=1, tiled=True),
    )
    outputs = []
    d_outputs = []
    sums = None
    for micro in range(micro_count):
        inputs = tokens[micro, 0].astype(jnp.float32)
        length = lengths[micro, 0]
        factor_attn = rms_scale(inputs)
        scaled_attn = inputs * factor_attn
        gain_one = held[3].astype(jnp.float32)
        normed_attn = (scaled_attn * gain_one).astype(jnp.bfloat16)
        mixed = plain_dot(normed_attn, held[0])
        query_low = mixed[:, :width].astype(jnp.bfloat16).reshape(slots, heads, head_size)
        key_low = mixed[:, width : 2 * width].astype(jnp.bfloat16)
        value_low = mixed[:, 2 * width :].astype(jnp.bfloat16)
        start_state = (
            jnp.full((heads, slots), NEGATIVE, jnp.float32),
            jnp.zeros((heads, slots), jnp.float32),
            jnp.zeros((slots, heads, head_size), jnp.float32),
        )
        top, total, accum = attend_forward(
            query_low,
            query_pos,
            length,
            padded,
            span,
            scale,
            start_state,
            lax.all_gather(key_low, "ctx", axis=0, tiled=True).reshape(-1, heads, head_size),
            lax.all_gather(value_low, "ctx", axis=0, tiled=True).reshape(-1, heads, head_size),
        )
        out_float = accum / total.T[:, :, None]
        lse = top + jnp.log(total)
        attended_low = out_float.reshape(slots, width).astype(jnp.bfloat16)
        resid = inputs + plain_dot(attended_low, held[1])
        factor_moe = rms_scale(resid)
        scaled_moe = resid * factor_moe
        gain_two = held[4].astype(jnp.float32)
        normed_moe = (scaled_moe * gain_two).astype(jnp.bfloat16)
        logits = plain_dot(normed_moe, held[2])
        chosen = (
            routes[micro, 0][:, :, None] == jnp.arange(experts, dtype=jnp.int32)[None, None, :]
        ).astype(jnp.float32)
        routed = jnp.sum(chosen * logits[:, None, :], axis=-1)
        gates = jax.nn.softmax(routed, axis=-1)
        weight_all = jnp.sum(chosen * gates[:, :, None], axis=1)
        final = resid
        hiddens = []
        actives = []
        results = []
        for expert in range(experts):
            hidden = plain_dot(normed_moe, held[5][expert])
            active = jax.nn.gelu(hidden, approximate=False).astype(jnp.bfloat16)
            result = plain_dot(active, held[6][expert])
            final = final + weight_all[:, expert : expert + 1] * result
            hiddens.append(hidden)
            actives.append(active)
            results.append(result)
        outputs.append(final.astype(jnp.bfloat16))
        valid = (query_pos < length).astype(jnp.float32)
        d_final = cotangent[micro, 0].astype(jnp.float32) * valid[:, None]
        d_norm_moe = jnp.zeros((slots, width), jnp.float32)
        grads_in = []
        grads_out = []
        d_gate_all = []
        for expert in range(experts):
            d_result = (weight_all[:, expert : expert + 1] * d_final).astype(jnp.bfloat16)
            grads_out.append(outer_dot(actives[expert], d_result))
            d_active = back_dot(d_result, held[6][expert])
            d_hidden = (d_active * gelu_slope(hiddens[expert])).astype(jnp.bfloat16)
            grads_in.append(outer_dot(normed_moe, d_hidden))
            d_norm_moe = d_norm_moe + back_dot(d_hidden, held[5][expert])
            d_gate_all.append(jnp.sum(d_final * results[expert], axis=-1))
        d_gate_all = jnp.stack(d_gate_all, axis=1)
        d_routed_gate = jnp.sum(chosen * d_gate_all[:, None, :], axis=-1)
        d_routed = gates * (d_routed_gate - jnp.sum(gates * d_routed_gate, axis=-1, keepdims=True))
        d_logits = jnp.sum(chosen * d_routed[:, :, None], axis=1).astype(jnp.bfloat16)
        grad_router = outer_dot(normed_moe, d_logits)
        d_norm_moe = d_norm_moe + back_dot(d_logits, held[2])
        d_resid_norm, grad_gain_moe = norm_back(d_norm_moe, scaled_moe, gain_two, factor_moe)
        d_resid = d_final + d_resid_norm
        d_branch = d_resid.astype(jnp.bfloat16)
        grad_attn = outer_dot(attended_low, d_branch)
        grad_low = back_dot(d_branch, held[1]).astype(jnp.bfloat16).reshape(slots, heads, head_size)
        key_whole, value_whole = (
            lax.all_gather(key_low, "ctx", axis=0, tiled=True),
            lax.all_gather(value_low, "ctx", axis=0, tiled=True),
        )
        d_query, d_dist, terms = attend_backward(
            query_low,
            grad_low,
            out_float,
            query_pos,
            length,
            padded,
            span,
            lse,
            scale,
            key_whole,
            value_whole,
        )
        owned = lax.psum_scatter(
            terms.astype(jnp.bfloat16), "ctx", scatter_dimension=0, tiled=True
        ).astype(jnp.float32)
        d_mixed = jnp.concatenate(
            [
                d_query.reshape(slots, width).astype(jnp.bfloat16),
                owned[:, :width].astype(jnp.bfloat16),
                owned[:, width:].astype(jnp.bfloat16),
            ],
            axis=1,
        )
        grad_qkv = outer_dot(normed_attn, d_mixed)
        d_norm_attn = back_dot(d_mixed, held[0])
        d_input_norm, grad_gain_attn = norm_back(d_norm_attn, scaled_attn, gain_one, factor_attn)
        d_outputs.append((d_resid + d_input_norm).astype(jnp.bfloat16))
        grad_bias = jnp.dot(buckets.T, d_dist.T, precision=HIGH).reshape(-1)
        grads = (
            grad_qkv,
            grad_attn,
            grad_router,
            grad_gain_attn,
            grad_gain_moe,
            jnp.stack(grads_in, axis=0),
            jnp.stack(grads_out, axis=0),
            grad_bias,
        )
        sums = grads if sums is None else jax.tree.map(jnp.add, sums, grads)
    sums = (
        lax.psum_scatter(sums[0], ("dp", "ctx"), scatter_dimension=0, tiled=True),
        lax.psum_scatter(sums[1], ("dp", "ctx"), scatter_dimension=0, tiled=True),
        lax.psum_scatter(sums[2], ("dp", "ctx"), scatter_dimension=0, tiled=True),
        lax.psum_scatter(sums[3], ("dp", "ctx"), scatter_dimension=0, tiled=True),
        lax.psum_scatter(sums[4], ("dp", "ctx"), scatter_dimension=0, tiled=True),
        lax.psum_scatter(sums[5], ("dp", "ctx"), scatter_dimension=1, tiled=True),
        lax.psum_scatter(sums[6], ("dp", "ctx"), scatter_dimension=1, tiled=True),
        lax.psum_scatter(sums[7], ("dp", "ctx"), scatter_dimension=0, tiled=True),
    )
    output = jnp.stack(outputs, axis=0)[:, None]
    d_tokens = jnp.stack(d_outputs, axis=0)[:, None]
    return (
        output,
        d_tokens,
        sums[0],
        sums[1],
        sums[2],
        sums[3],
        sums[4],
        sums[5],
        sums[6],
        sums[7],
    )


def solution(mesh):
    in_specs = (
        P(None, "dp", "ctx", None),
        P(None, "dp"),
        P(None, "dp", "ctx", None),
        P(),
        P(),
        P(None, "dp", "ctx", None),
        P("dp", None),
        P("dp", None),
        P("dp", None),
        P("dp"),
        P("dp"),
        P(None, "dp", None),
        P(None, "dp", None),
    )
    out_specs = (
        P(None, "dp", "ctx", None),
        P(None, "dp", "ctx", None),
        P(("dp", "ctx"), None),
        P(("dp", "ctx"), None),
        P(("dp", "ctx"), None),
        P(("dp", "ctx")),
        P(("dp", "ctx")),
        P(None, ("dp", "ctx"), None),
        P(None, ("dp", "ctx"), None),
        P(("dp", "ctx")),
    )
    return jax.shard_map(local, mesh=mesh, in_specs=in_specs, out_specs=out_specs, check_vma=False)
```

profile of v0, /device:TPU:0, one launch (start us, length us, event | category | flops | bytes accessed | tf_op | source)
XLA Modules:
  0.0 1962.3 jit_solution(4359083302487049786)
XLA Ops:
  11.6 11.9 all-reduce.12
  25.2 34.7 %all-gather.10.cloned.1.call-done = bf16[768,2304]{1,0:T(8,128)(2,1)} async-done(((bf16[192,2304]{1,0:T(8,128)(2,1)}), bf16[768,2304]{1,0:T(8,128)(2,1)}) %all-gather.10.cloned.1.call-update) | async-done | bytes 3538960 | tf_op jit(solution)/shard_map/all_gather | solution.py:236
  70.3 8.0 all-gather
  93.3 22.4 %all-gather.14.cloned.1.call-done = bf16[1024,768]{1,0:T(8,128)(2,1)} async-done(((bf16[128,768]{1,0:T(8,128)(2,1)}), bf16[1024,768]{1,0:T(8,128)(2,1)}) %all-gather.14.cloned.1.call-update) | async-done | bytes 1572880 | tf_op jit(solution)/shard_map/all_gather | solution.py:272
  120.1 22.3 %all-gather.22.cloned.1.call-done = bf16[1024,768]{1,0:T(8,128)(2,1)} async-done(((bf16[128,768]{1,0:T(8,128)(2,1)}), bf16[1024,768]{1,0:T(8,128)(2,1)}) %all-gather.22.cloned.1.call-update) | async-done | bytes 1572880 | tf_op jit(solution)/shard_map/all_gather | solution.py:271
  146.8 22.3 %all-gather.24.cloned.1.call-done = bf16[1024,768]{1,0:T(8,128)(2,1)} async-done(((bf16[128,768]{1,0:T(8,128)(2,1)}), bf16[1024,768]{1,0:T(8,128)(2,1)}) %all-gather.24.cloned.1.call-update) | async-done | bytes 1572880 | tf_op jit(solution)/shard_map/all_gather | solution.py:272
  175.4 45.8 %while.60 = (s32[]{:T(128)}, f32[12,128]{1,0:T(8,128)S(1)}, f32[12,128]{1,0:T(8,128)}, f32[128,12,64]{0,2,1:T(8,128)}, s32[2]{0:T(128)}, /*index=5*/s32[]{:T(128...) while((s32[]{:T(128)}, f32[12,128]{1,0:T(8,128)S(1)}, ...), condition=%wide.region_7.8_spmd.clone, body=%wide.region_1.7_spmd.clone.sunk | while | flops 209598080 | bytes 65464984 | solution.py:116
  180.6 35.9 %conditional.12 = ((f32[12,128]{1,0:T(8,128)S(1)}, f32[12,128]{1,0:T(8,128)}, f32[128,12,64]{0,2,1:T(8,128)})) conditional(s32[]{:T(128)} %convert_element_type.685, (f32[12,128]{1,0:T(8,128)S(1)}, f32[12,128]{1,0:T(8,128)}, f32[128,12,64]{0,2,1:T(8,128)}) %tuple.227, (pred[128,512]{0,1:T(8,128)(4,1)}, bf16[2,512,12,64]{1,3,2,0:T(8,128)(2,1)}, ...), branch_computations={%region_3.3_spmd, %region_4.6_spmd} | conditional | flops 209399808 | bytes 65393012 | solution.py:114
  196.1 7.3 reshape.534
  227.2 42.8 %while.61 = (s32[]{:T(128)}, f32[12,128]{1,0:T(8,128)S(1)}, f32[12,128]{1,0:T(8,128)}, f32[128,12,64]{0,2,1:T(8,128)}, s32[2]{0:T(128)}, /*index=5*/s32[]{:T(128...) while((s32[]{:T(128)}, f32[12,128]{1,0:T(8,128)S(1)}, ...), condition=%wide.region_20.21_spmd.clone, body=%wide.region_14.20_spmd.clone.sunk | while | flops 209598080 | bytes 65202808 | solution.py:116
  231.4 34.4 %conditional.13 = ((f32[12,128]{1,0:T(8,128)S(1)}, f32[12,128]{1,0:T(8,128)}, f32[128,12,64]{0,2,1:T(8,128)})) conditional(s32[]{:T(128)} %convert_element_type.686, (f32[12,128]{1,0:T(8,128)S(1)}, f32[12,128]{1,0:T(8,128)}, f32[128,12,64]{0,2,1:T(8,128)}) %tuple.231, (pred[128,512]{0,1:T(8,128)(4,1)S(1)}, bf16[2,512,12,64]{1,3,2,0:T(8,128)(2,1)}, ...), branch_computations={%region_16.16_spmd, %region_17.19_spmd} | conditional | flops 209399808 | bytes 65130840 | solution.py:114
  246.9 7.3 reshape.535
  275.4 100.1 %all-gather.18.cloned.1.call-done = bf16[4,768,3072]{2,1,0:T(8,128)(2,1)} async-done(((bf16[4,192,3072]{2,1,0:T(8,128)(2,1)}), bf16[4,768,3072]{2,1,0:T(8,128)(2,1)}) %all-gather.18.cloned.1.call-update) | async-done | bytes 18874384 | tf_op jit(solution)/shard_map/all_gather | solution.py:241
  375.5 7.5 fusion.136
  419.0 133.9 %all-gather.20.cloned.1.call-done = bf16[4,3072,768]{2,1,0:T(8,128)(2,1)} async-done(((bf16[4,768,768]{2,1,0:T(8,128)(2,1)}), bf16[4,3072,768]{2,1,0:T(8,128)(2,1)}) %all-gather.20.cloned.1.call-update) | async-done | bytes 18874384 | tf_op jit(solution)/shard_map/all_gather | solution.py:242
  642.7 87.6 %while.62 = (s32[]{:T(128)}, f32[128,12,64]{0,2,1:T(8,128)}, f32[12,4096]{1,0:T(8,128)}, bf16[2,512,1536]{2,1,0:T(8,128)(2,1)}, s32[2]{0:T(128)S(1)}, /*index=5*...) while((s32[]{:T(128)}, f32[128,12,64]{0,2,1:T(8,128)}, ...), condition=%wide.region_40.41_spmd.clone, body=%wide.region_35.40_spmd.clone.sunk | while | flops 515913344 | bytes 129618840 | solution.py:193
  647.0 71.9 %conditional.14 = (f32[128,12,64]{0,2,1:T(8,128)}, f32[12,4096]{1,0:T(8,128)}, bf16[1,512,1536]{1,2,0:T(8,128)(2,1)}) conditional(s32[]{:T(128)} %convert_element_type.687, (f32[128,12,64]{0,2,1:T(8,128)}, f32[12,4096]{1,0:T(8,128)}) %tuple.235, (pred[128,512]{0,1:T(8,128)(4,1)}, bf16[2,512,12,64]{1,3,2,0:T(8,128)(2,1)}, s32[]{:T(128)}, ...), branch_computations={%region_37.37_spmd, %region_38.39_spmd} | conditional | flops 515715072 | bytes 123254752 | solution.py:190
  662.6 7.3 reshape.536
  686.7 6.5 reshape.537
  697.6 6.9 reshape.557
  737.5 99.7 %while.63 = (s32[]{:T(128)}, f32[128,12,64]{0,2,1:T(8,128)}, f32[12,4096]{1,0:T(8,128)}, bf16[2,512,1536]{2,1,0:T(8,128)(2,1)}, s32[2]{0:T(128)S(1)}, /*index=5*...) while((s32[]{:T(128)}, f32[128,12,64]{0,2,1:T(8,128)}, ...), condition=%wide.region_57.58_spmd.clone, body=%wide.region_52.57_spmd.clone.sunk | while | flops 515913344 | bytes 129618840 | solution.py:193
  753.6 72.0 %conditional.15 = (f32[128,12,64]{0,2,1:T(8,128)}, f32[12,4096]{1,0:T(8,128)}, bf16[1,512,1536]{1,2,0:T(8,128)(2,1)}) conditional(s32[]{:T(128)} %convert_element_type.688, (f32[128,12,64]{0,2,1:T(8,128)}, f32[12,4096]{1,0:T(8,128)}) %tuple.239, (pred[128,512]{0,1:T(8,128)(4,1)}, bf16[2,512,12,64]{1,3,2,0:T(8,128)(2,1)}, s32[]{:T(128)}, ...), branch_computations={%region_54.54_spmd, %region_55.56_spmd} | conditional | flops 515715072 | bytes 123254752 | solution.py:190
  769.1 7.3 reshape.542
  793.3 6.5 reshape.543
  804.2 6.9 reshape.559
  848.4 170.8 %reduce-scatter.10.cloned.1.call-done = bf16[128,1536]{1,0:T(8,128)(2,1)} async-done(((bf16[1024,1536]{1,0:T(8,128)(2,1)}), bf16[128,1536]{1,0:T(8,128)(2,1)}) %reduce-scatter.10.cloned.1.call-update) | async-done | bytes 393232 | tf_op jit(solution)/shard_map/reduce_scatter | solution.py:344
  1019.2 7.2 convolution_add_fusion
  1067.9 39.0 %maximum_add_fusion = f32[4,768,3072]{2,1,0:T(8,128)} fusion(f32[1,768,3072]{2,1,0:T(8,128)} %convolution_bitcast_fusion.12, f32[1,768,3072]{2,1,0:T(8,128)} %convolution_bitcast_fusion.13, f32[1,768,3072]{2,1,0:T(8,128)} %convolution_bitcast_fusion.14, f32[1,768,3072]{2,1,0:T(8,128)} %convolution_bitcast_fusion.15, ...), kind=kLoop, calls=%fused_computation.130 | loop fusion | flops 66060288 | bytes 113246208 | tf_op jit(solution)/shard_map/add | solution.py:370
  1149.0 40.3 %maximum_add_fusion.1 = f32[4,3072,768]{2,1,0:T(8,128)} fusion(f32[1,3072,768]{2,1,0:T(8,128)} %convolution_bitcast_fusion.4, f32[1,3072,768]{2,1,0:T(8,128)} %convolution_bitcast_fusion.5, f32[1,3072,768]{2,1,0:T(8,128)} %convolution_bitcast_fusion.6, f32[1,3072,768]{2,1,0:T(8,128)} %convolution_bitcast_fusion.7, ...), kind=kLoop, calls=%fused_computation.131 | loop fusion | flops 66060288 | bytes 113246208 | tf_op jit(solution)/shard_map/add | solution.py:370
  1205.8 39.3 %all-reduce.11 = (f32[768,4]{0,1:T(4,128)S(1)}, f32[768]{0:T(1024)S(1)}, f32[768]{0:T(1024)S(1)}, f32[384]{0:T(512)S(1)}) all-reduce(f32[768,4]{0,1:T(4,128)} %convolution_add_fusion.6, f32[768]{0:T(1024)S(1)} %add.487, f32[768]{0:T(1024)S(1)} %add.488, f32[384]{0:T(512)} %add.492), channel_id=6, replica_groups=mesh['dp'=4,'ctx'=8] {'dp','ctx'}, use_global_device_ids=true, to_apply=%region_62.63.clone | all-reduce | flops 4992 | bytes 39936
  1251.4 350.2 %reduce-scatter.16.cloned.1.call-done = f32[4,24,3072]{2,1,0:T(8,128)} async-done(((f32[4,768,3072]{2,1,0:T(8,128)}), f32[4,24,3072]{2,1,0:T(8,128)}) %reduce-scatter.16.cloned.1.call-update) | async-done | bytes 1179664 | tf_op jit(solution)/shard_map/reduce_scatter | solution.py:377
  1601.6 353.9 %reduce-scatter.18.cloned.1.call-done = f32[4,96,768]{2,1,0:T(8,128)} async-done(((f32[4,3072,768]{2,1,0:T(8,128)}), f32[4,96,768]{2,1,0:T(8,128)}) %reduce-scatter.18.cloned.1.call-update) | async-done | bytes 1179664 | tf_op jit(solution)/shard_map/reduce_scatter | solution.py:378
  (671 shorter events, 503.5 us)
Async XLA Ops:
  7.2 71.8 %copy-start = (f32[32,12]{0,1:T(8,128)S(1)}, f32[32,12]{0,1:T(8,128)}, u32[]{:S(2)}) copy-start(f32[32,12]{0,1:T(8,128)} %param.33) | copy-start | bytes 4612
  7.2 52.7 %all-gather.10.cloned.1.call-start = ((), (), s32[]{:S(2)}) async-start(), calls=%async_computation.6 | async-start | bytes 4423680 | tf_op jit(solution)/shard_map/all_gather | solution.py:236
  7.9 80.9 %all-gather.12.cloned.1.call-start = ((), (), s32[]{:S(2)}) async-start(), calls=%async_computation.7 | async-start | bytes 1769472 | tf_op jit(solution)/shard_map/all_gather | solution.py:271
  23.5 41.0 %copy-start.90 = (f32[768]{0:T(1024)}, f32[768]{0:T(1024)S(1)}, u32[]{:S(2)}) copy-start(f32[768]{0:T(1024)S(1)} %convert_element_type.327) | copy-start | bytes 9220
  25.2 37.6 %copy-start.104 = (f32[128]{0:T(128)}, f32[128]{0:T(128)S(1)}, u32[]{:S(2)}) copy-start(f32[128]{0:T(128)S(1)} %get-tuple-element.1337) | copy-start | bytes 1540
  63.7 52.1 %all-gather.14.cloned.1.call-start = ((), (), s32[]{:S(2)}) async-start(), calls=%async_computation.8 | async-start | bytes 1769472 | tf_op jit(solution)/shard_map/all_gather | solution.py:272
  64.4 78.0 %all-gather.22.cloned.1.call-start = ((), (), s32[]{:S(2)}) async-start(), calls=%async_computation.12 | async-start | bytes 1769472 | tf_op jit(solution)/shard_map/all_gather | solution.py:271
  66.9 102.2 %all-gather.24.cloned.1.call-start = ((), (), s32[]{:S(2)}) async-start(), calls=%async_computation.13 | async-start | bytes 1769472 | tf_op jit(solution)/shard_map/all_gather | solution.py:272
  67.5 154.8 %all-gather.16.cloned.1.call-start = ((), (), s32[]{:S(2)}) async-start(), calls=%async_computation.9 | async-start | bytes 1474560 | tf_op jit(solution)/shard_map/all_gather | solution.py:237
  68.1 307.4 %all-gather.18.cloned.1.call-start = ((), (), s32[]{:S(2)}) async-start(), calls=%async_computation.10 | async-start | bytes 23592960 | tf_op jit(solution)/shard_map/all_gather | solution.py:241
  68.9 484.0 %all-gather.20.cloned.1.call-start = ((), (), s32[]{:S(2)}) async-start(), calls=%async_computation.11 | async-start | bytes 23592960 | tf_op jit(solution)/shard_map/all_gather | solution.py:242
  69.6 773.6 %reduce-scatter.8.cloned.1.call-start = ((), (), s32[]{:S(2)}) async-start(), calls=%async_computation.14 | async-start | bytes 3538944 | tf_op jit(solution)/shard_map/reduce_scatter | solution.py:344
  273.5 109.5 %copy-start.115 = (f32[128]{0:T(128)}, f32[128]{0:T(128)S(1)}, u32[]{:S(2)}) copy-start(f32[128]{0:T(128)S(1)} %add_rsqrt_fusion) | copy-start | bytes 1540
  275.0 133.5 %copy-start.25 = (bf16[128,768]{1,0:T(8,128)(2,1)}, bf16[128,768]{1,0:T(8,128)(2,1)S(1)}, u32[]{:S(2)}) copy-start(bf16[128,768]{1,0:T(8,128)(2,1)S(1)} %get-tuple-element.1301) | copy-start | bytes 589828
  275.1 138.5 %copy-start.27 = (bf16[128,768]{1,0:T(8,128)(2,1)}, bf16[128,768]{1,0:T(8,128)(2,1)S(1)}, u32[]{:S(2)}) copy-start(bf16[128,768]{1,0:T(8,128)(2,1)S(1)} %get-tuple-element.1300) | copy-start | bytes 589828
  383.9 186.0 %copy-start.41 = (bf16[128,3072]{1,0:T(8,128)(2,1)}, bf16[128,3072]{1,0:T(8,128)(2,1)S(1)}, u32[]{:S(2)}) copy-start(bf16[128,3072]{1,0:T(8,128)(2,1)S(1)} %get-tuple-element.1332) | copy-start | bytes 2359300
  403.7 160.0 %copy-start.43 = (bf16[128,3072]{1,0:T(8,128)(2,1)}, bf16[128,3072]{1,0:T(8,128)(2,1)S(1)}, u32[]{:S(2)}) copy-start(bf16[128,3072]{1,0:T(8,128)(2,1)S(1)} %get-tuple-element.1326) | copy-start | bytes 2359300
  408.6 159.1 %copy-start.45 = (bf16[128,3072]{1,0:T(8,128)(2,1)}, bf16[128,3072]{1,0:T(8,128)(2,1)S(1)}, u32[]{:S(2)}) copy-start(bf16[128,3072]{1,0:T(8,128)(2,1)S(1)} %get-tuple-element.1328) | copy-start | bytes 2359300
  572.4 30.0 %copy-start.117 = (f32[128]{0:T(128)}, f32[128]{0:T(128)S(1)}, u32[]{:S(2)}) copy-start(f32[128]{0:T(128)S(1)} %get-tuple-element.1308) | copy-start | bytes 1540
  572.4 30.0 %copy-start.119 = (f32[128]{0:T(128)}, f32[128]{0:T(128)S(1)}, u32[]{:S(2)}) copy-start(f32[128]{0:T(128)S(1)} %get-tuple-element.1311) | copy-start | bytes 1540
  572.4 30.0 %copy-start.121 = (f32[128]{0:T(128)}, f32[128]{0:T(128)S(1)}, u32[]{:S(2)}) copy-start(f32[128]{0:T(128)S(1)} %get-tuple-element.1310) | copy-start | bytes 1540
  572.4 30.0 %copy-start.123 = (f32[128]{0:T(128)}, f32[128]{0:T(128)S(1)}, u32[]{:S(2)}) copy-start(f32[128]{0:T(128)S(1)} %get-tuple-element.1309) | copy-start | bytes 1540
  604.2 29.9 %copy-start.125 = (f32[128]{0:T(128)}, f32[128]{0:T(128)S(1)}, u32[]{:S(2)}) copy-start(f32[128]{0:T(128)S(1)} %get-tuple-element.1302) | copy-start | bytes 1540
  604.2 29.9 %copy-start.127 = (f32[128]{0:T(128)}, f32[128]{0:T(128)S(1)}, u32[]{:S(2)}) copy-start(f32[128]{0:T(128)S(1)} %get-tuple-element.1305) | copy-start | bytes 1540
  730.4 288.8 %reduce-scatter.10.cloned.1.call-start = ((), (), s32[]{:S(2)}) async-start(), calls=%async_computation.15 | async-start | bytes 3538944 | tf_op jit(solution)/shard_map/reduce_scatter | solution.py:344
  837.3 414.1 %reduce-scatter.14.cloned.1.call-start = ((), (), s32[]{:S(2)}) async-start(), calls=%async_computation.17 | async-start | bytes 2433024 | tf_op jit(solution)/shard_map/reduce_scatter | solution.py:373
  840.7 410.7 %reduce-scatter.12.cloned.1.call-start = ((), (), s32[]{:S(2)}) async-start(), calls=%async_computation.16 | async-start | bytes 7299072 | tf_op jit(solution)/shard_map/reduce_scatter | solution.py:372
  842.0 177.2 %copy-start.35 = (bf16[128,768]{1,0:T(8,128)(2,1)}, bf16[128,768]{1,0:T(8,128)(2,1)S(1)}, u32[]{:S(2)}) copy-start(bf16[128,768]{1,0:T(8,128)(2,1)S(1)} %copy.223) | copy-start | bytes 589828
  843.2 176.0 %copy-start.111 = (f32[128]{0:T(128)S(1)}, f32[128]{0:T(128)}, u32[]{:S(2)}) copy-start(f32[128]{0:T(128)} %get-tuple-element.1336) | copy-start | bytes 1540
  1026.4 575.1 %reduce-scatter.16.cloned.1.call-start = ((), (), s32[]{:S(2)}) async-start(), calls=%async_computation.18 | async-start | bytes 38928384 | tf_op jit(solution)/shard_map/reduce_scatter | solution.py:377
  1106.9 848.6 %reduce-scatter.18.cloned.1.call-start = ((), (), s32[]{:S(2)}) async-start(), calls=%async_computation.19 | async-start | bytes 38928384 | tf_op jit(solution)/shard_map/reduce_scatter | solution.py:378
  1248.8 706.7 %copy-start.1 = (f32[32,12]{0,1:T(8,128)S(1)}, f32[32,12]{0,1:T(8,128)}, u32[]{:S(2)}) copy-start(f32[32,12]{0,1:T(8,128)} %param.33) | copy-start | bytes 4612
  (151 other events, 741.1 us)
Sparse Core Ops, SparseCore 0:
  9.9 49.9 all-gather.9
  63.8 25.0 all-gather.11
  91.1 24.5 all-gather.13
  117.8 24.5 all-gather.21
  144.5 24.5 all-gather.23
  170.8 27.2 all-gather.15
  199.9 175.4 all-gather.17
  377.3 175.4 all-gather.19
  730.5 111.0 reduce-scatter.7
  843.7 175.4 reduce-scatter.9
  1025.1 98.0 reduce-scatter.13
  1130.2 118.3 reduce-scatter.11
  1255.6 345.9 reduce-scatter.15
  1609.6 345.9 reduce-scatter.17
where the time goes:
time: 1970 us; the launch traced here: 1960 us
  waiting for transfers between devices  1220 us (62%)
  matrix products  265 us (13%)
  local copies, waits for them, and re-layouts  231 us (12%)
  other arithmetic  145 us (7%)
  blocking collectives  59.2 us (3%)
  loops' own time  24.9 us (1%)
    reduce_scatter x1, waiting for transfers between devices, local(): lax.psum_scatter(sums[6], ('dp', 'ctx'), scatter_dimension=1, tiled=True)  354 us
    reduce_scatter x1, waiting for transfers between devices, local(): lax.psum_scatter(sums[5], ('dp', 'ctx'), scatter_dimension=1, tiled=True)  350 us
    reduce_scatter x2, waiting for transfers between devices, local(): lax.psum_scatter(terms.astype(jnp.bfloat16), 'ctx', scatter_dimension=0,...  171 us
    all_gather x1, waiting for transfers between devices, local(): lax.all_gather(w_expert_out, 'dp', axis=1, tiled=True)  134 us
    all_gather x1, waiting for transfers between devices, local(): lax.all_gather(w_expert_in, 'dp', axis=1, tiled=True)  100 us
    dot_general x22, matrix products, outer_dot(): lax.dot_general(left, right, (((0,), (0,)), ((), ())), preferred_element_...  98.3 us
    add x4, other arithmetic, local(): sums = grads if sums is None else jax.tree.map(jnp.add, sums, grads)  79.3 us
    dot_general x22, matrix products, plain_dot(): return jnp.dot(left, right, preferred_element_type=jnp.float32)  70.4 us
  transfers between devices with their start and end apart: 14, of which 10 were waited for; matrix products, arithmetic and copies ran while one was open for 23% of the time, Pallas kernels for 0%

commit v1 on v0

v1 whole, which is shorter than its diff:
```python
import functools

import jax
import jax.numpy as jnp
from jax import lax
from jax.experimental import pallas as pl
from jax.experimental.pallas import tpu as pltpu
from jax.sharding import PartitionSpec as P

EPSILON = 1e-06
NEGATIVE = -1e30
HIGH = lax.Precision.HIGHEST
F32 = jnp.float32
BF16 = jnp.bfloat16
PLANE = ("dp", "core")
COLUMN = ("z", "core")
EVERY = ("dp", "z", "core")
VMEM_LIMIT = 60 * 1024 * 1024


def dot_nn(left, right):
    return lax.dot_general(left, right, (((1,), (0,)), ((), ())), preferred_element_type=F32)


def dot_nt(left, right):
    return lax.dot_general(left, right, (((1,), (1,)), ((), ())), preferred_element_type=F32)


def dot_tn(left, right):
    return lax.dot_general(left, right, (((0,), (0,)), ((), ())), preferred_element_type=F32)


def rms_scale(values):
    return lax.rsqrt(jnp.mean(values * values, axis=-1, keepdims=True) + EPSILON)


def norm_back(grad, scaled, gain, factor):
    inner = grad * gain
    return (
        factor * (inner - scaled * jnp.mean(inner * scaled, axis=-1, keepdims=True)),
        jnp.sum(grad * scaled, axis=0),
    )


def bias_tile(rd_ref, head, delta, span, block):
    low = span - (delta + 1) * block
    row = rd_ref[head : head + 1, low : low + 2 * block]
    wide = jnp.broadcast_to(row, (block, 2 * block))
    return pltpu.roll(wide, block + 1, 1, stride=1, stride_axis=0)[:, :block]


def allowed_tile(length, first_query, first_key, block):
    query = first_query + lax.broadcasted_iota(jnp.int32, (block, block), 0)
    key = first_key + lax.broadcasted_iota(jnp.int32, (block, block), 1)
    allowed = key < length
    if first_query == first_key:
        allowed = allowed & (key <= query)
    return allowed


def attend_kernel(
    len_ref, x_ref, gain_ref, w_ref, rd_ref, n1_ref, qkv_ref, o_ref, olow_ref, lse_ref, tb_ref,
    *, hg, hd, block, scale,
):
    span = x_ref.shape[0]
    count = span // block
    width = hg * hd
    length = len_ref[0]
    gain = gain_ref[...].astype(F32)
    for i in range(count):
        rows = slice(i * block, (i + 1) * block)
        x = x_ref[rows, :].astype(F32)
        n1 = (x * rms_scale(x) * gain).astype(BF16)
        n1_ref[rows, :] = n1
        qkv_ref[rows, :] = dot_nn(n1, w_ref[...]).astype(BF16)
    for head in range(hg):
        for delta in range(count):
            tb_ref[head, delta] = bias_tile(rd_ref, head, delta, span, block)
    lane = lax.broadcasted_iota(jnp.int32, (block, 128), 1)
    for i in range(count):
        rows = slice(i * block, (i + 1) * block)
        lse_all = jnp.zeros((block, 128), F32)
        outs = []
        for head in range(hg):
            cols = slice(head * hd, (head + 1) * hd)
            kcols = slice(width + head * hd, width + (head + 1) * hd)
            vcols = slice(2 * width + head * hd, 2 * width + (head + 1) * hd)
            q = qkv_ref[rows, cols]
            scores = []
            top = None
            for j in range(i + 1):
                keys = slice(j * block, (j + 1) * block)
                s = dot_nt(q, qkv_ref[keys, kcols]) * scale + tb_ref[head, i - j]
                s = jnp.where(allowed_tile(length, i * block, j * block, block), s, NEGATIVE)
                scores.append(s)
                peak = jnp.max(s, axis=-1, keepdims=True)
                top = peak if top is None else jnp.maximum(top, peak)
            total = jnp.zeros((block, 1), F32)
            accum = jnp.zeros((block, hd), F32)
            for j in range(i + 1):
                keys = slice(j * block, (j + 1) * block)
                weights = jnp.exp(scores[j] - top)
                total = total + jnp.sum(weights, axis=-1, keepdims=True)
                accum = accum + dot_nn(weights.astype(BF16), qkv_ref[keys, vcols])
            outs.append(accum / total)
            lse_all = jnp.where(lane == head, top + jnp.log(total), lse_all)
        out = jnp.concatenate(outs, axis=1)
        o_ref[rows, :] = out
        olow_ref[rows, :] = out.astype(BF16)
        lse_ref[rows, :] = lse_all


def vmem_specs(count):
    return [pl.BlockSpec(memory_space=pltpu.VMEM)] * count


def attend(length, x_all, gain, w, rd, hg, hd, scale):
    span, model = x_all.shape
    block = 256
    width = hg * hd
    return pl.pallas_call(
        functools.partial(attend_kernel, hg=hg, hd=hd, block=block, scale=scale),
        out_shape=(
            jax.ShapeDtypeStruct((span, model), BF16),
            jax.ShapeDtypeStruct((span, 3 * width), BF16),
            jax.ShapeDtypeStruct((span, width), F32),
            jax.ShapeDtypeStruct((span, width), BF16),
            jax.ShapeDtypeStruct((span, 128), F32),
        ),
        in_specs=[pl.BlockSpec(memory_space=pltpu.SMEM)] + vmem_specs(4),
        out_specs=tuple(vmem_specs(5)),
        scratch_shapes=[pltpu.VMEM((hg, span // block, block, block), F32)],
        compiler_params=pltpu.CompilerParams(vmem_limit_bytes=VMEM_LIMIT),
        name="attend",
    )(length, x_all, gain, w, rd)


def skew_sum(tile):
    rows, wide = tile.shape
    while rows > 1:
        half = rows // 2
        tile = tile[:half] + pltpu.roll(tile[half:], wide - half, 1)
        rows = half
    return tile


def attend_back_kernel(
    len_ref, n1_ref, qkv_ref, o_ref, lse_ref, do_ref, w_ref, rd_ref,
    dn1_ref, dw_ref, dd_ref, tb_ref, dt_ref, dacc_ref, dlow_ref,
    *, hg, hd, block, scale,
):
    span = n1_ref.shape[0]
    count = span // block
    width = hg * hd
    length = len_ref[0]
    for head in range(hg):
        for delta in range(count):
            tb_ref[head, delta] = bias_tile(rd_ref, head, delta, span, block)
    dt_ref[...] = jnp.zeros_like(dt_ref)
    dacc_ref[...] = jnp.zeros_like(dacc_ref)
    for i in range(count):
        rows = slice(i * block, (i + 1) * block)
        for head in range(hg):
            cols = slice(head * hd, (head + 1) * hd)
            kcols = slice(width + head * hd, width + (head + 1) * hd)
            vcols = slice(2 * width + head * hd, 2 * width + (head + 1) * hd)
            q = qkv_ref[rows, cols]
            do = do_ref[rows, cols]
            delta_sum = jnp.sum(do.astype(F32) * o_ref[rows, cols], axis=-1, keepdims=True)
            lse = lse_ref[rows, head : head + 1]
            dq = jnp.zeros((block, hd), F32)
            for j in range(i + 1):
                keys = slice(j * block, (j + 1) * block)
                k = qkv_ref[keys, kcols]
                s = dot_nt(q, k) * scale + tb_ref[head, i - j]
                p = jnp.exp(s - lse)
                p = jnp.where(allowed_tile(length, i * block, j * block, block), p, 0.0)
                dp = dot_nt(do, qkv_ref[keys, vcols])
                ds = (p * (dp - delta_sum)).astype(BF16)
                dt_ref[head, i - j] += ds.astype(F32)
                dq = dq + dot_nn(ds, k)
                dacc_ref[keys, kcols] += dot_tn(ds, q)
                dacc_ref[keys, vcols] += dot_tn(p.astype(BF16), do)
            dacc_ref[rows, cols] = dq
    for i in range(count):
        rows = slice(i * block, (i + 1) * block)
        dlow_ref[rows, : 2 * width] = (dacc_ref[rows, : 2 * width] * scale).astype(BF16)
        dlow_ref[rows, 2 * width :] = dacc_ref[rows, 2 * width :].astype(BF16)
        dn1_ref[rows, :] = dot_nt(dlow_ref[rows, :], w_ref[...]).astype(BF16)
    dw_ref[...] = dot_tn(n1_ref[...], dlow_ref[...]).astype(dw_ref.dtype)
    dd_ref[...] = jnp.zeros_like(dd_ref)
    for head in range(hg):
        for delta in range(count):
            low = span - (delta + 1) * block
            tile = jnp.concatenate(
                [dt_ref[head, delta], jnp.zeros((block, block), F32)], axis=1
            )
            row = pltpu.roll(skew_sum(tile), block - 1, 1)
            dd_ref[head : head + 1, low : low + 2 * block] += row


def attend_back(length, n1, qkv, o, lse, do, w, rd, hg, hd, scale):
    span, model = n1.shape
    block = 256
    width = hg * hd
    return pl.pallas_call(
        functools.partial(attend_back_kernel, hg=hg, hd=hd, block=block, scale=scale),
        out_shape=(
            jax.ShapeDtypeStruct((span, model), BF16),
            jax.ShapeDtypeStruct((model, 3 * width), BF16),
            jax.ShapeDtypeStruct((hg, span + block), F32),
        ),
        in_specs=[pl.BlockSpec(memory_space=pltpu.SMEM)] + vmem_specs(7),
        out_specs=tuple(vmem_specs(3)),
        scratch_shapes=[
            pltpu.VMEM((hg, span // block, block, block), F32),
            pltpu.VMEM((hg, span // block, block, block), F32),
            pltpu.VMEM((span, 3 * width), F32),
            pltpu.VMEM((span, 3 * width), BF16),
        ],
        compiler_params=pltpu.CompilerParams(vmem_limit_bytes=VMEM_LIMIT),
        name="attend_back",
    )(length, n1, qkv, o, lse, do, w, rd)


def gelu_parts(hidden):
    density = jnp.exp(-0.5 * hidden * hidden)
    t = 1.0 / (1.0 + (0.3275911 * 0.7071067811865476) * jnp.abs(hidden))
    poly = 1.061405429 * t - 1.453152027
    poly = poly * t + 1.421413741
    poly = poly * t - 0.284496736
    poly = poly * t + 0.254829592
    tail = 0.5 * poly * t * density
    phi = jnp.where(hidden >= 0.0, 1.0 - tail, tail)
    return hidden * phi, phi + hidden * density * 0.3989422804014327


def expert_kernel(
    n2_ref, dy_ref, c_ref, win_ref, wout_ref, y_ref, dn2_ref, dg_ref, dwin_ref, dwout_ref,
    awin_ref, awout_ref, *, experts, hidden_count,
):
    step = pl.program_id(0)
    last = pl.num_programs(0) - 1

    @pl.when(step == 0)
    def start():
        awin_ref[...] = jnp.zeros_like(awin_ref)
        awout_ref[...] = jnp.zeros_like(awout_ref)

    n2 = n2_ref[...]
    dy = dy_ref[...]
    c = c_ref[...]
    dgs = []
    y = None
    dn2 = None
    for e in range(experts):
        part = slice(e * hidden_count, (e + 1) * hidden_count)
        weight = c[:, e : e + 1]
        hidden = dot_nn(n2, win_ref[:, part])
        active, slope = gelu_parts(hidden)
        back = dot_nt(dy, wout_ref[part, :])
        dgs.append(jnp.sum(active * back, axis=-1, keepdims=True))
        mixed = (active * weight).astype(BF16)
        d_hidden = (back * weight * slope).astype(BF16)
        term = dot_nn(mixed, wout_ref[part, :])
        y = term if y is None else y + term
        term = dot_nt(d_hidden, win_ref[:, part])
        dn2 = term if dn2 is None else dn2 + term
        awout_ref[part, :] += dot_tn(mixed, dy)
        awin_ref[:, part] += dot_tn(n2, d_hidden)
    y_ref[...] = y.astype(BF16)
    dn2_ref[...] = dn2.astype(BF16)
    dg_ref[...] = jnp.concatenate(dgs, axis=1)

    @pl.when(step == last)
    def finish():
        dwin_ref[...] = awin_ref[...].astype(BF16)
        dwout_ref[...] = awout_ref[...].astype(BF16)


def expert_layer(n2, dy, c, win, wout, experts):
    count, model = n2.shape
    block = 256
    hidden_count = win.shape[1] // experts
    rows = pl.BlockSpec((block, model), lambda i: (i, 0))
    few = pl.BlockSpec((block, experts), lambda i: (i, 0))
    whole = pl.BlockSpec(memory_space=pltpu.VMEM)
    return pl.pallas_call(
        functools.partial(expert_kernel, experts=experts, hidden_count=hidden_count),
        out_shape=(
            jax.ShapeDtypeStruct((count, model), BF16),
            jax.ShapeDtypeStruct((count, model), BF16),
            jax.ShapeDtypeStruct((count, experts), F32),
            jax.ShapeDtypeStruct(win.shape, BF16),
            jax.ShapeDtypeStruct(wout.shape, BF16),
        ),
        grid=(count // block,),
        in_specs=[rows, rows, few, whole, whole],
        out_specs=(rows, rows, few, whole, whole),
        scratch_shapes=[pltpu.VMEM(win.shape, F32), pltpu.VMEM(wout.shape, F32)],
        compiler_params=pltpu.CompilerParams(vmem_limit_bytes=VMEM_LIMIT),
        name="experts",
    )(n2, dy, c, win, wout)


def local(
    tokens, lengths, routes, rel_table, rel_bias, cotangent, w_qkv, w_attn, w_router,
    gain_attn, gain_moe, w_expert_in, w_expert_out, *, ndp, nz,
):
    micro, _, slots, model = tokens.shape
    span = rel_table.shape[0]
    buckets_count, heads = rel_bias.shape
    hd = model // heads
    scale = hd ** (-0.5)
    experts = w_expert_in.shape[0]
    ff = w_expert_in.shape[2]
    hg = -(-heads // nz)
    pad_heads = hg * nz - heads
    width = hg * hd
    z = lax.axis_index("z")
    core = lax.axis_index("core")
    x_loc = tokens[:, 0]
    query_pos = (z * 2 + core) * slots + jnp.arange(slots, dtype=jnp.int32)
    valid = query_pos[None, :] < lengths
    dy_loc = jnp.where(valid[:, :, None], cotangent[:, 0], 0).reshape(micro * slots, model)

    x_all = lax.all_to_all(x_loc, "core", 0, 1, tiled=True)[0]
    x_all = lax.all_gather(x_all, "z", axis=0, tiled=True)
    wq = w_qkv.reshape(-1, 3, heads, hd)
    wq = jnp.pad(wq, ((0, 0), (0, 0), (0, pad_heads), (0, 0)))
    wq = lax.dynamic_slice_in_dim(wq, z * hg, hg, 2).reshape(-1, 3 * width)
    wq = lax.all_gather(wq, "dp", axis=0, tiled=True)
    wa = lax.all_gather(w_attn, "dp", axis=0, tiled=True)
    wr = lax.all_gather(w_router, "dp", axis=0, tiled=True)
    ga = lax.all_gather(gain_attn, "dp", axis=0, tiled=True)
    gm = lax.all_gather(gain_moe, "dp", axis=0, tiled=True)
    share = ff // (ndp * nz * 2)
    hidden_count = nz * share
    win = w_expert_in.reshape(experts, -1, ndp, nz, 2, share)
    win = lax.dynamic_index_in_dim(win, core, 4, keepdims=False)
    win = win.transpose(2, 1, 0, 3, 4).reshape(ndp, -1, experts * hidden_count)
    win = lax.all_to_all(win, "dp", 0, 0, tiled=True).reshape(model, experts * hidden_count)
    wout = w_expert_out.reshape(experts, nz, 2, share, model)
    wout = lax.dynamic_index_in_dim(wout, core, 2, keepdims=False)
    wout = wout.reshape(experts * hidden_count, model)
    dy = lax.all_gather(dy_loc, PLANE, axis=0, tiled=True)

    turned = rel_table[::-1]
    onehot = (turned[:, None] == jnp.arange(buckets_count, dtype=jnp.int32)[None, :]).astype(F32)
    bias_rows = jnp.pad(rel_bias.T, ((0, pad_heads), (0, 0)))
    bias_rows = lax.dynamic_slice_in_dim(bias_rows, z * hg, hg, 0)
    rd = lax.dot_general(bias_rows, onehot, (((1,), (1,)), ((), ())), precision=HIGH)
    rd = jnp.pad(rd, ((0, 0), (0, 256)))
    length = lax.dynamic_index_in_dim(lengths[:, 0], core, 0, keepdims=True)

    n1, qkv, o, olow, lse = attend(length, x_all, ga[None, :], wq, rd, hg, hd, scale)
    olow = olow.reshape(nz * 2, slots, width)
    olow = lax.all_to_all(olow, COLUMN, 0, 0, tiled=True)
    olow = olow.reshape(nz, 2, slots, width).transpose(1, 2, 0, 3)
    olow = olow.reshape(micro * slots, nz * width)[:, :model]

    x = x_loc.reshape(micro * slots, model).astype(F32)
    y1 = x + dot_nn(olow, wa)
    r2 = rms_scale(y1)
    z2 = y1 * r2
    gain_two = gm.astype(F32)
    n2 = (z2 * gain_two).astype(BF16)
    logits = dot_nn(n2, wr)
    chosen = (
        routes.reshape(micro * slots, 2)[:, :, None] == jnp.arange(experts)[None, None, :]
    ).astype(F32)
    routed = jnp.sum(chosen * logits[:, None, :], axis=-1)
    gates = jax.nn.softmax(routed, axis=-1)
    c = jnp.sum(chosen * gates[:, :, None], axis=1)

    n2_all = lax.all_gather(n2, PLANE, axis=0, tiled=True)
    c_all = lax.all_gather(c, PLANE, axis=0, tiled=True)
    y_part, dn2_part, dg_part, dwin, dwout = expert_layer(n2_all, dy, c_all, win, wout, experts)
    y = lax.psum_scatter(y_part, PLANE, scatter_dimension=0, tiled=True)
    dn2 = lax.psum_scatter(dn2_part, PLANE, scatter_dimension=0, tiled=True).astype(F32)
    dg = lax.psum_scatter(dg_part, PLANE, scatter_dimension=0, tiled=True)
    output = (y1 + y.astype(F32)).astype(BF16)

    d_routed_gate = jnp.sum(chosen * dg[:, None, :], axis=-1)
    d_routed = gates * (d_routed_gate - jnp.sum(gates * d_routed_gate, axis=-1, keepdims=True))
    d_logits = jnp.sum(chosen * d_routed[:, :, None], axis=1).astype(BF16)
    g_router = dot_tn(n2, d_logits)
    dn2 = dn2 + dot_nt(d_logits, wr)
    d_norm, g_gain_moe = norm_back(dn2, z2, gain_two, r2)
    dy1 = dy_loc.astype(F32) + d_norm
    dbr = dy1.astype(BF16)
    g_attn = dot_tn(olow, dbr).astype(BF16)
    do = dot_nt(dbr, wa).astype(BF16)
    do = jnp.pad(do, ((0, 0), (0, nz * width - model)))
    do = do.reshape(2, slots, nz, width).transpose(2, 0, 1, 3).reshape(nz * 2, slots, width)
    do = lax.all_to_all(do, COLUMN, 0, 0, tiled=True).reshape(span, width)

    dn1_part, g_qkv, dd = attend_back(length, n1, qkv, o, lse, do, wq, rd, hg, hd, scale)
    dn1 = dn1_part.reshape(nz, 1, 2 * slots, model)
    dn1 = lax.psum_scatter(dn1, "z", scatter_dimension=0, tiled=True)[0]
    dn1 = lax.all_to_all(dn1, "core", 1, 0, tiled=True).reshape(micro * slots, model).astype(F32)
    r1 = rms_scale(x)
    z1 = x * r1
    d_norm, g_gain_attn = norm_back(dn1, z1, ga.astype(F32), r1)
    d_tokens = (dy1 + d_norm).astype(BF16)

    piece = model // (ndp * nz * 2)
    g_out = lax.psum_scatter(
        dwout.reshape(experts, nz, share, model), "z", scatter_dimension=1, tiled=True
    ).reshape(experts, share, model).astype(F32)
    g_in = dwin.reshape(ndp, nz, 2, piece, experts * hidden_count)
    g_in = lax.psum_scatter(g_in, "z", scatter_dimension=1, tiled=True)
    g_in = g_in.reshape(ndp * 2, piece, experts * hidden_count)
    g_in = lax.all_to_all(g_in, PLANE, 0, 0, tiled=True)
    g_in = g_in.reshape(ndp, 2, piece, experts, nz, share).transpose(3, 2, 0, 4, 1, 5)
    g_in = g_in.reshape(experts, piece, ff).astype(F32)
    g_qkv = g_qkv.reshape(ndp, nz, 2, piece, 3 * width).transpose(0, 2, 1, 3, 4)
    g_qkv = g_qkv.reshape(ndp * 2, nz, piece, 3 * width)
    g_qkv = lax.psum_scatter(g_qkv, PLANE, scatter_dimension=0, tiled=True)[0]
    g_qkv = lax.all_to_all(g_qkv, "z", 0, 0, tiled=True)
    g_qkv = g_qkv.reshape(nz, piece, 3, width).transpose(1, 2, 0, 3).reshape(piece, 3, nz * width)
    g_qkv = g_qkv[:, :, :model].reshape(piece, 3 * model).astype(F32)
    g_attn = lax.psum_scatter(g_attn, EVERY, scatter_dimension=0, tiled=True).astype(F32)

    d_dist = dd[:, :span]
    g_bias = lax.dot_general(onehot, d_dist, (((0,), (1,)), ((), ())), precision=HIGH)
    spread = jnp.zeros((buckets_count, nz * hg), F32)
    g_bias = lax.dynamic_update_slice_in_dim(spread, g_bias, z * hg, 1)[:, :heads].reshape(-1)
    small = jnp.concatenate([g_router.reshape(-1), g_gain_attn, g_gain_moe, g_bias])
    small = lax.psum(small, EVERY)
    place = (lax.axis_index("dp") * nz + z) * 2 + core

    def own(first, count, rows):
        return lax.dynamic_slice_in_dim(small, first + place * rows, rows, 0)

    g_router = own(0, 0, piece * experts).reshape(piece, experts)
    g_gain_attn = own(model * experts, 0, piece)
    g_gain_moe = own(model * (experts + 1), 0, piece)
    each = buckets_count * heads // (ndp * nz * 2)
    g_bias = own(model * (experts + 2), 0, each)
    return (
        output.reshape(micro, 1, slots, model),
        d_tokens.reshape(micro, 1, slots, model),
        g_qkv, g_attn, g_router, g_gain_attn, g_gain_moe, g_in, g_out, g_bias,
    )


def solution(mesh):
    devices = mesh.devices
    ndp, nctx = devices.shape
    nz = nctx // 2
    sub = jax.sharding.Mesh(devices.reshape(ndp, nz, 2), EVERY)
    in_specs = (
        P(None, "dp", COLUMN, None),
        P(None, "dp"),
        P(None, "dp", COLUMN, None),
        P(),
        P(),
        P(None, "dp", COLUMN, None),
        P("dp", None),
        P("dp", None),
        P("dp", None),
        P("dp"),
        P("dp"),
        P(None, "dp", None),
        P(None, "dp", None),
    )
    out_specs = (
        P(None, "dp", COLUMN, None),
        P(None, "dp", COLUMN, None),
        P(EVERY, None),
        P(EVERY, None),
        P(EVERY, None),
        P(EVERY),
        P(EVERY),
        P(None, EVERY, None),
        P(None, EVERY, None),
        P(EVERY),
    )
    return jax.shard_map(
        functools.partial(local, ndp=ndp, nz=nz), mesh=sub,
        in_specs=in_specs, out_specs=out_specs, check_vma=False,
    )
```

time: 1970 us -> 768 us (0.39)
  waiting for transfers between devices: 1220 us -> 396 us
  matrix products: 265 us -> 8.39 us
  local copies, waits for them, and re-layouts: 231 us -> 74.9 us
  other arithmetic: 145 us -> 17.1 us
  blocking collectives: 59.2 us -> 148 us
  Pallas kernels: 0 us -> 81.9 us
  loops' own time: 24.9 us -> 0 us
    reduce_scatter x6 -> x7, waiting for transfers between devices: 875 us -> 316 us  [the longest x1 95.6 us: local(): lax.psum_scatter(g_attn, EVERY, scatter_dimension=0, tiled=True).astype(F32)]
    all_gather x8 -> x4, waiting for transfers between devices: 340 us -> 7.9 us  [the longest x1 7.87 us: local(): x_all = lax.all_gather(x_all, 'z', axis=0, tiled=True)]
    dot_general x83 -> x8, matrix products: 265 us -> 8.39 us  [the longest x2 3.4 us: dot_nt(): lax.dot_general(left, right, (((1,), (1,)), ((), ())), preferred_element_...]
    add x27 -> x2, other arithmetic: 88.6 us -> 2.42 us  [the longest x1 2.42 us: local(): dy1 = dy_loc.astype(F32) + d_norm]
    pallas_call x0 -> x3, Pallas kernels: none -> 81.9 us  [the longest x1 50.6 us: expert_layer(): pl.pallas_call(functools.partial(expert_kernel, experts=experts, hidden_c...]
    all_gather x1 -> x3, blocking collectives: 8.02 us -> 59.6 us  [the longest x1 36.6 us: local(): wr = lax.all_gather(w_router, 'dp', axis=0, tiled=True)]
    unnamed x14 -> x13, waiting for transfers between devices: 3.94 us -> 52.1 us
    another operation x24 -> x0, local copies, waits for them, and re-layouts: 47.6 us -> none  [the longest x8 33.3 us: bias_block(): flat = jnp.tile(rolled, (1, queries))[:, :queries * (extent - 1)]]
  transfers between devices with their start and end apart: 14 -> 16, of which waited for: 10 -> 11; matrix products, arithmetic and copies ran while one was open for 23% -> 11% of each run, Pallas kernels for 0% -> 4%
where the time goes in v1:
time: 768 us; the launch traced here: 760 us
  waiting for transfers between devices  396 us (52%)
  blocking collectives  148 us (19%)
  Pallas kernels  81.9 us (11%)
  local copies, waits for them, and re-layouts  74.9 us (10%)
  starting transfers between devices  17.4 us (2%)
  other arithmetic  17.1 us (2%)
  between operations  16 us (2%)
  matrix products  8.39 us (1%)
    reduce_scatter x1, waiting for transfers between devices, local(): lax.psum_scatter(g_attn, EVERY, scatter_dimension=0, tiled=True).astype(F32)  95.6 us
    unnamed x13, waiting for transfers between devices  52.1 us
    pallas_call x1, Pallas kernels, expert_layer(): pl.pallas_call(functools.partial(expert_kernel, experts=experts, hidden_c...  50.6 us
    reduce_scatter x1, waiting for transfers between devices, local(): lax.psum_scatter(dn2_part, PLANE, scatter_dimension=0, tiled=True)  48.4 us
    reduce_scatter x1, waiting for transfers between devices, local(): y = lax.psum_scatter(y_part, PLANE, scatter_dimension=0, tiled=True)  47.1 us
    psum x1, blocking collectives, local(): small = lax.psum(small, EVERY)  39.3 us
    all_gather x1, blocking collectives, local(): wr = lax.all_gather(w_router, 'dp', axis=0, tiled=True)  36.6 us
    reduce_scatter x1, waiting for transfers between devices, local(): g_qkv = lax.psum_scatter(g_qkv, PLANE, scatter_dimension=0, tiled=True)[0]  36.1 us
  transfers between devices with their start and end apart: 16, of which 11 were waited for; matrix products, arithmetic and copies ran while one was open for 11% of the time, Pallas kernels for 4%

profile of v1, /device:TPU:0, one launch (start us, length us, event | category | flops | bytes accessed | tf_op | source)
XLA Modules:
  0.0 759.6 jit_solution(2075135101333570381)
XLA Ops:
  7.3 6.1 all_to_all.43
  20.1 11.3 %all-reduce.4 = (bf16[768]{0:T(1024)(128)(2,1)S(1)}, bf16[768]{0:T(1024)(128)(2,1)S(1)}) all-reduce(bf16[768]{0:T(1024)(128)(2,1)S(1)} %dynamic-update-slice, bf16[768]{0:T(1024)(128)(2,1)S(1)} %dynamic-update-slice.1), channel_id=1, replica_groups=mesh['dp'=4,'z'=4,'core'=2] {'dp'}, use_global_device_ids=true, to_apply=%add.1 | all-reduce | flops 1536 | bytes 6144
  33.7 11.8 %all_gather.29.w_ref = bf16[768,576]{1,0:T(8,128)(2,1)} all-gather(bf16[192,576]{1,0:T(8,128)(2,1)S(1)} %copy.119), channel_id=1, replica_groups=mesh['dp'=4,'z'=4,'core'=2] {'dp'}, dimensions={0}, use_global_device_ids=true | all-gather | bytes 1105920 | tf_op jit(solution)/shard_map/all_gather | solution.py:332
  45.4 7.9 %all-gather.6.cloned.1.call-done.x_ref = bf16[1024,768]{1,0:T(8,128)(2,1)} async-done(((bf16[256,768]{1,0:T(8,128)(2,1)}), bf16[1024,768]{1,0:T(8,128)(2,1)}) %all-gather.6.cloned.1.call-update) | async-done | bytes 1572880 | tf_op jit(solution)/shard_map/all_gather | solution.py:328
  53.3 10.6 %attend.1 = (bf16[1024,768]{1,0:T(8,128)(2,1)}, bf16[1024,576]{1,0:T(8,128)(2,1)}, f32[1024,192]{1,0:T(8,128)}, bf16[1024,192]{1,0:T(8,128)(2,1)}, f32[1024,128]{1,0:T(8,128)}) custom-call(s32[1]{0:T(128)} %bitcast.1.len_ref, bf16[1024,768]{1,0:T(8,128)(2,1)} %all-gather.6.cloned.1.call-done.x_ref, bf16[1,768]{1,0:T(2,128)(2,1)} %broadcast_in_dim.16.gain_ref, ...), custom_call_target="tpu_custom_call" | custom-call | tf_op jit(solution)/shard_map/attend/pallas_call | solution.py:121
  65.9 3.5 all-to-all-start.1
  70.0 11.8 %all-to-all-done.1 = bf16[8,128,192]{1,2,0:T(8,128)(2,1)S(1)} async-done(((bf16[8,128,192]{1,2,0:T(8,128)(2,1)}), bf16[8,128,192]{1,2,0:T(8,128)(2,1)S(1)}, u32[]{:S(2)}, u32[]{:S(2)}) %all-to-all-start.1) | async-done | bytes 393248 | tf_op jit(solution)/shard_map/all_to_all | solution.py:358
  86.1 19.6 %reshape.342 = bf16[4,192,4,4,2,96]{5,4,3,2,1,0:T(2,128)(2,1)} reshape(bf16[4,192,3072]{2,1,0:T(8,128)(2,1)} %param.24) | data formatting | bytes 9437184 | tf_op jit(solution)/shard_map/reshape | solution.py:339
  105.7 7.8 %constant_dynamic-slice_fusion.1 = bf16[4,192,4,4,1,96]{5,4,3,2,1,0:T(2,128)(2,1)S(1)} fusion(bf16[4,192,4,4,2,96]{5,4,3,2,1,0:T(2,128)(2,1)} %reshape.342, s32[]{:T(128)S(6)} %select_n.30), kind=kLoop, calls=%fused_computation.51 | loop fusion | bytes 4718596 | tf_op jit(solution)/shard_map/jit(dynamic_index_in_dim)/dynamic_slice | solution.py:340
  118.0 4.5 reshape.343
  122.5 3.8 all-to-all-start.2
  126.3 36.6 %all-gather = bf16[4,192,4]{1,2,0:T(4,128)(2,1)S(1)} all-gather(bf16[1,192,4]{1,2,0:T(4,128)(2,1)S(1)} %bitcast.146), channel_id=1, replica_groups=mesh['dp'=4,'z'=4,'core'=2] {'dp'}, dimensions={0}, use_global_device_ids=true | all-gather | bytes 7680 | tf_op jit(solution)/shard_map/all_gather | solution.py:334
  163.0 3.3 constant_dynamic-slice_fusion
  166.8 11.3 %all_gather.35.c_ref = f32[2048,4]{1,0:T(8,128)} all-gather(f32[256,4]{1,0:T(8,128)S(1)} %copy.123), channel_id=1, replica_groups=mesh['dp'=4,'z'=4,'core'=2] {'dp','core'}, dimensions={0}, use_global_device_ids=true | all-gather | bytes 36864 | tf_op jit(solution)/shard_map/all_gather | solution.py:377
  179.5 50.6 %experts.1 = (bf16[2048,768]{1,0:T(8,128)(2,1)}, bf16[2048,768]{1,0:T(8,128)(2,1)}, f32[2048,4]{1,0:T(8,128)}, bf16[768,1536]{1,0:T(8,128)(2,1)}, bf16[1536,768]{1,0:T(8,128)(2,1)}) custom-call(bf16[2048,768]{1,0:T(8,128)(2,1)} %all-gather.10.cloned.1.call-done.n2_ref, bf16[2048,768]{1,0:T(8,128)(2,1)} %all-gather.12.cloned.1.call-done.dy_ref, ...), custom_call_target="tpu_custom_call" | custom-call | tf_op jit(solution)/shard_map/experts/pallas_call | solution.py:288
  234.1 31.4 %reduce-scatter.15.cloned.1.call-done = f32[256,4]{1,0:T(8,128)} async-done(((f32[2048,4]{1,0:T(8,128)}), f32[256,4]{1,0:T(8,128)}) %reduce-scatter.15.cloned.1.call-update) | async-done | bytes 4112 | tf_op jit(solution)/shard_map/reduce_scatter | solution.py:381
  266.6 48.4 %reduce-scatter.13.cloned.1.call-done = bf16[256,768]{1,0:T(8,128)(2,1)} async-done(((bf16[2048,768]{1,0:T(8,128)(2,1)}), bf16[256,768]{1,0:T(8,128)(2,1)}) %reduce-scatter.13.cloned.1.call-update) | async-done | bytes 393232 | tf_op jit(solution)/shard_map/reduce_scatter | solution.py:380
  317.9 47.1 %reduce-scatter.11.cloned.1.call-done = bf16[256,768]{1,0:T(8,128)(2,1)} async-done(((bf16[2048,768]{1,0:T(8,128)(2,1)}), bf16[256,768]{1,0:T(8,128)(2,1)}) %reduce-scatter.11.cloned.1.call-update) | async-done | bytes 393232 | tf_op jit(solution)/shard_map/reduce_scatter | solution.py:379
  368.3 27.2 %all_to_all.44 = bf16[8,128,192]{1,2,0:T(8,128)(2,1)S(1)} all-to-all(bf16[8,128,192]{1,2,0:T(8,128)(2,1)S(1)} %bitcast.132), channel_id=1, replica_groups=mesh['dp'=4,'z'=4,'core'=2] {'z','core'}, dimensions={0} | all-to-all | bytes 786432 | tf_op jit(solution)/shard_map/all_to_all | solution.py:396
  396.5 20.7 %attend_back.1 = (bf16[1024,768]{1,0:T(8,128)(2,1)}, bf16[768,576]{1,0:T(8,128)(2,1)}, f32[3,1280]{1,0:T(4,128)}) custom-call(s32[1]{0:T(128)} %bitcast.1.len_ref, bf16[1024,768]{1,0:T(8,128)(2,1)} %get-tuple-element.27.n1_ref, bf16[1024,576]{1,0:T(8,128)(2,1)} %get-tuple-element.28.qkv_ref, f32[1024,192]{1,0:T(8,128)} %get-tuple-element.29.o_ref, ...), custom_call_target="tpu_custom_call" | custom-call | tf_op jit(solution)/shard_map/attend_back/pallas_call | solution.py:206
  422.3 48.9 %all-reduce.7.cloned.1.call-done = bf16[4,4,2,24,1536]{4,3,2,1,0:T(8,128)(2,1)} async-done(((bf16[4,4,2,24,1536]{4,3,2,1,0:T(8,128)(2,1)}), bf16[4,4,2,24,1536]{4,3,2,1,0:T(8,128)(2,1)}) %all-reduce.7.cloned.1.call-update) | async-done | bytes 2359312
  473.7 4.2 all-to-all-start.6
  479.8 8.6 %all-to-all-done.6 = bf16[8,24,1536]{2,1,0:T(8,128)(2,1)} async-done(((bf16[8,24,1536]{2,1,0:T(8,128)(2,1)}), bf16[8,24,1536]{2,1,0:T(8,128)(2,1)}, u32[]{:S(2)}, u32[]{:S(2)}) %all-to-all-start.6) | async-done | bytes 589856 | tf_op jit(solution)/shard_map/all_to_all | solution.py:414
  493.1 3.9 reshape.365
  497.0 23.6 %reduce-scatter.23.cloned.1.call-done = bf16[4,1,96,768]{3,2,0,1:T(8,128)(2,1)} async-done(((bf16[4,4,96,768]{3,2,0,1:T(8,128)(2,1)}), bf16[4,1,96,768]{3,2,0,1:T(8,128)(2,1)}) %reduce-scatter.23.cloned.1.call-update) | async-done | bytes 589840 | tf_op jit(solution)/shard_map/reduce_scatter | solution.py:408
  522.7 36.1 %reduce-scatter.19.cloned.1.call-done = bf16[1,4,24,576]{3,2,1,0:T(8,128)(2,1)} async-done(((bf16[8,4,24,576]{3,2,1,0:T(8,128)(2,1)}), bf16[1,4,24,576]{3,2,1,0:T(8,128)(2,1)}) %reduce-scatter.19.cloned.1.call-update) | async-done | bytes 110608 | tf_op jit(solution)/shard_map/reduce_scatter | solution.py:419
  558.9 4.9 all-to-all-start.5
  565.3 95.6 %reduce-scatter.21.cloned.1.call-done = bf16[24,768]{1,0:T(8,128)(2,1)} async-done(((bf16[768,768]{1,0:T(8,128)(2,1)}), bf16[24,768]{1,0:T(8,128)(2,1)}) %reduce-scatter.21.cloned.1.call-update) | async-done | bytes 36880 | tf_op jit(solution)/shard_map/reduce_scatter | solution.py:423
  663.7 33.9 %reduce-scatter.17.cloned.1.call-done = bf16[1,1,256,768]{3,2,1,0:T(8,128)(2,1)} async-done(((bf16[4,1,256,768]{3,2,1,0:T(8,128)(2,1)}), bf16[1,1,256,768]{3,2,1,0:T(8,128)(2,1)}) %reduce-scatter.17.cloned.1.call-update) | async-done | bytes 393232 | tf_op jit(solution)/shard_map/reduce_scatter | solution.py:400
  699.8 3.1 reduce.6
  703.0 4.0 all_to_all.45
  709.2 39.3 %psum.7 = f32[4992]{0:T(1024)S(1)} all-reduce(f32[4992]{0:T(1024)S(1)} %pad_maximum_fusion), channel_id=1, replica_groups=mesh['dp'=4,'z'=4,'core'=2] {'dp','z','core'}, use_global_device_ids=true, to_apply=%region_19.20 | all-reduce | flops 4992 | bytes 39936 | tf_op jit(solution)/shard_map/psum | solution.py:430
  (173 shorter events, 62.4 us)
Async XLA Ops:
  7.2 25.4 %copy-start = (f32[32,12]{0,1:T(8,128)S(1)}, f32[32,12]{0,1:T(8,128)}, u32[]{:S(2)}) copy-start(f32[32,12]{0,1:T(8,128)} %param.17) | copy-start | bytes 4612
  7.2 9.6 %copy-start.21 = (s32[1024]{0:T(1024)S(1)}, s32[1024]{0:T(1024)}, u32[]{:S(2)}) copy-start(s32[1024]{0:T(1024)} %param.16) | copy-start | bytes 12292
  7.2 9.7 %copy-start.13 = (bf16[192,2304]{1,0:T(8,128)(2,1)S(1)}, bf16[192,2304]{1,0:T(8,128)(2,1)}, u32[]{:S(2)}) copy-start(bf16[192,2304]{1,0:T(8,128)(2,1)} %param.19) | copy-start | bytes 2654212
  7.2 46.1 %all-gather.6.cloned.1.call-start = ((), (), s32[]{:S(2)}) async-start(), calls=%async_computation.14 | async-start | bytes 1966080 | tf_op jit(solution)/shard_map/all_gather | solution.py:328
  13.4 6.5 copy-start.28
  13.4 68.9 %all-gather.8.cloned.1.call-start = ((), (), s32[]{:S(2)}) async-start(), calls=%async_computation.15 | async-start | bytes 1474560 | tf_op jit(solution)/shard_map/all_gather | solution.py:333
  14.2 163.9 %all-gather.12.cloned.1.call-start = ((), (), s32[]{:S(2)}) async-start(), calls=%async_computation.17 | async-start | bytes 3538944 | tf_op jit(solution)/shard_map/all_gather | solution.py:346
  16.9 16.7 %copy-start.22 = (s32[1024]{0:T(1024)}, s32[1024]{0:T(1024)S(1)}, u32[]{:S(2)}) copy-start(s32[1024]{0:T(1024)S(1)} %rev.3) | copy-start | bytes 12292
  45.4 24.5 %copy-start.8 = (bf16[2,1,128,768]{3,2,1,0:T(8,128)(2,1)S(1)}, bf16[2,1,128,768]{3,2,1,0:T(8,128)(2,1)}, u32[]{:S(2)}) copy-start(bf16[2,1,128,768]{3,2,1,0:T(8,128)(2,1)} %param.13) | copy-start | bytes 1179652
  65.9 15.9 %all-to-all-start.1 = ((bf16[8,128,192]{1,2,0:T(8,128)(2,1)}), bf16[8,128,192]{1,2,0:T(8,128)(2,1)S(1)}, u32[]{:S(2)}, u32[]{:S(2)}) async-start(bf16[8,128,192]{1,2,0:T(8,128)(2,1)} %copy.120), calls=%async_computation.1 | async-start | bytes 786432 | tf_op jit(solution)/shard_map/all_to_all | solution.py:358
  69.4 108.7 %all-gather.10.cloned.1.call-start = ((), (), s32[]{:S(2)}) async-start(), calls=%async_computation.16 | async-start | bytes 3538944 | tf_op jit(solution)/shard_map/all_gather | solution.py:376
  70.0 16.1 %copy-start.5 = (f32[2,1,128,768]{3,2,1,0:T(8,128)}, f32[2,1,128,768]{3,2,1,0:T(8,128)S(1)}, u32[]{:S(2)}) copy-start(f32[2,1,128,768]{3,2,1,0:T(8,128)S(1)} %convert_element_type.146) | copy-start | bytes 2359300
  84.3 21.4 %copy-start.16 = (f32[256]{0:T(256)}, f32[256]{0:T(256)S(1)}, u32[]{:S(2)}) copy-start(f32[256]{0:T(256)S(1)} %add_rsqrt_fusion) | copy-start | bytes 3076
  122.5 55.6 %all-to-all-start.2 = ((bf16[4,192,1536]{2,1,0:T(8,128)(2,1)}), bf16[4,192,1536]{2,1,0:T(8,128)(2,1)S(1)}, u32[]{:S(2)}, u32[]{:S(2)}) async-start(bf16[4,192,1536]{2,1,0:T(8,128)(2,1)} %reshape.343), calls=%async_computation.2 | async-start | bytes 4718592 | tf_op jit(solution)/shard_map/all_to_all | solution.py:342
  126.3 139.3 %reduce-scatter.15.cloned.1.call-start = ((), (), s32[]{:S(2)}) async-start(), calls=%async_computation.20 | async-start | bytes 1179648 | tf_op jit(solution)/shard_map/reduce_scatter | solution.py:381
  230.1 84.9 %reduce-scatter.13.cloned.1.call-start = ((), (), s32[]{:S(2)}) async-start(), calls=%async_computation.19 | async-start | bytes 3538944 | tf_op jit(solution)/shard_map/reduce_scatter | solution.py:380
  230.7 134.3 %reduce-scatter.11.cloned.1.call-start = ((), (), s32[]{:S(2)}) async-start(), calls=%async_computation.18 | async-start | bytes 3538944 | tf_op jit(solution)/shard_map/reduce_scatter | solution.py:379
  231.4 239.7 %all-reduce.7.cloned.1.call-start = ((), (), s32[]{:S(2)}) async-start(), calls=%async_computation.25 | async-start | bytes 4718592
  232.2 288.4 %reduce-scatter.23.cloned.1.call-start = ((), (), s32[]{:S(2)}) async-start(), calls=%async_computation.24 | async-start | bytes 2949120 | tf_op jit(solution)/shard_map/reduce_scatter | solution.py:408
  234.0 81.0 %copy-start.3 = (f32[256,768]{1,0:T(8,128)S(1)}, f32[256,768]{1,0:T(8,128)}, u32[]{:S(2)}) copy-start(f32[256,768]{1,0:T(8,128)} %copy-done.2) | copy-start | bytes 2359300
  234.0 81.0 %copy-start.17 = (f32[256]{0:T(256)S(1)}, f32[256]{0:T(256)}, u32[]{:S(2)}) copy-start(f32[256]{0:T(256)} %copy-done.16) | copy-start | bytes 3076
  234.0 324.8 %reduce-scatter.19.cloned.1.call-start = ((), (), s32[]{:S(2)}) async-start(), calls=%async_computation.22 | async-start | bytes 1105920 | tf_op jit(solution)/shard_map/reduce_scatter | solution.py:419
  266.6 100.8 %copy-start.9 = (bf16[768,768]{1,0:T(8,128)(2,1)S(1)}, bf16[768,768]{1,0:T(8,128)(2,1)}, u32[]{:S(2)}) copy-start(bf16[768,768]{1,0:T(8,128)(2,1)} %all-gather.8.cloned.1.call-done) | copy-start | bytes 3538948
  419.5 241.5 %reduce-scatter.21.cloned.1.call-start = ((), (), s32[]{:S(2)}) async-start(), calls=%async_computation.23 | async-start | bytes 1216512 | tf_op jit(solution)/shard_map/reduce_scatter | solution.py:423
  421.1 57.0 %copy-start.19 = (bf16[768]{0:T(1024)(128)(2,1)S(1)}, bf16[768]{0:T(1024)(128)(2,1)}, u32[]{:S(2)}) copy-start(bf16[768]{0:T(1024)(128)(2,1)} %copy-done.18) | copy-start | bytes 4612
  421.1 276.5 %reduce-scatter.17.cloned.1.call-start = ((), (), s32[]{:S(2)}) async-start(), calls=%async_computation.21 | async-start | bytes 1966080 | tf_op jit(solution)/shard_map/reduce_scatter | solution.py:400
  473.7 14.7 %all-to-all-start.6 = ((bf16[8,24,1536]{2,1,0:T(8,128)(2,1)}), bf16[8,24,1536]{2,1,0:T(8,128)(2,1)}, u32[]{:S(2)}, u32[]{:S(2)}) async-start(bf16[8,24,1536]{2,1,0:T(8,128)(2,1)} %bitcast.40), calls=%async_computation.12 | async-start | bytes 1179648 | tf_op jit(solution)/shard_map/all_to_all | solution.py:414
  493.1 70.7 %copy-start.23 = (s32[1024]{0:T(1024)S(1)}, s32[1024]{0:T(1024)}, u32[]{:S(2)}) copy-start(s32[1024]{0:T(1024)} %copy-done.22) | copy-start | bytes 12292
  493.1 70.7 %copy-start.26 = (f32[3,1280]{1,0:T(4,128)S(1)}, f32[3,1280]{1,0:T(4,128)}, u32[]{:S(2)}) copy-start(f32[3,1280]{1,0:T(4,128)} %get-tuple-element.33) | copy-start | bytes 46084
  558.9 103.5 %all-to-all-start.5 = ((bf16[4,24,576]{2,1,0:T(8,128)(2,1)}), bf16[4,24,576]{2,1,0:T(8,128)(2,1)S(1)}, u32[]{:S(2)}, u32[]{:S(2)}) async-start(bf16[4,24,576]{2,1,0:T(8,128)(2,1)} %bitcast.141), calls=%async_computation.10 | async-start | bytes 245760 | tf_op jit(solution)/shard_map/all_to_all | solution.py:420
  697.6 9.9 %copy-start.6 = (f32[2,1,128,768]{3,2,1,0:T(8,128)S(1)}, f32[2,1,128,768]{3,2,1,0:T(8,128)}, u32[]{:S(2)}) copy-start(f32[2,1,128,768]{3,2,1,0:T(8,128)} %copy-done.5) | copy-start | bytes 2359300
  703.0 49.3 %copy-start.1 = (f32[32,12]{0,1:T(8,128)S(1)}, f32[32,12]{0,1:T(8,128)}, u32[]{:S(2)}) copy-start(f32[32,12]{0,1:T(8,128)} %param.17) | copy-start | bytes 4612
  (15 other events, 47.5 us)
Sparse Core Ops, SparseCore 0:
  13.5 39.7 all-gather.5
  55.1 26.5 all-gather.7
  84.2 32.3 all-gather.11
  118.9 49.3 all-gather.9
  230.2 35.2 reduce-scatter.14
  268.8 46.1 reduce-scatter.12
  318.7 46.2 reduce-scatter.10
  367.4 103.7 all-reduce.6
  473.5 47.0 reduce-scatter.22
  523.6 35.2 reduce-scatter.18
  564.8 96.1 reduce-scatter.20
  663.2 34.2 reduce-scatter.16

commit v2 on v1

--- a/solution.py
+++ b/solution.py
@@ -58,26 +58,171 @@
     return allowed
 
 
-def attend_kernel(
-    len_ref, x_ref, gain_ref, w_ref, rd_ref, n1_ref, qkv_ref, o_ref, olow_ref, lse_ref, tb_ref,
-    *, hg, hd, block, scale,
+MESH = pl.DeviceIdType.MESH
+
+
+def xor(left, right):
+    out = 0
+    bit = 1
+    while bit <= right:
+        here = lax.rem(lax.div(left, jnp.int32(bit)), jnp.int32(2))
+        out = out + bit * (1 - here if right & bit else here)
+        bit *= 2
+    return out + lax.div(left, jnp.int32(bit)) * bit
+
+
+def remote(source, target, send, receive, dp, z, core):
+    return pltpu.make_async_remote_copy(
+        src_ref=source, dst_ref=target, send_sem=send, recv_sem=receive,
+        device_id={"dp": dp, "z": z, "core": core}, device_id_type=MESH,
+    )
+
+
+def gate_weights(logits, routes, experts):
+    lane = lax.broadcasted_iota(jnp.int32, logits.shape, 1).astype(F32)
+    first = lane == routes[:, 0:1]
+    second = lane == routes[:, 1:2]
+    one = jnp.sum(jnp.where(first, logits, 0.0), axis=-1, keepdims=True)
+    two = jnp.sum(jnp.where(second, logits, 0.0), axis=-1, keepdims=True)
+    top = jnp.maximum(one, two)
+    one = jnp.exp(one - top)
+    two = jnp.exp(two - top)
+    scale = 1.0 / (one + two)
+    return jnp.where(first, one * scale, 0.0) + jnp.where(second, two * scale, 0.0)
+
+
+def front_kernel(
+    len_ref, x_ref, cot_ref, route_ref, rd_ref, wq_l, wa_l, small_l, win_h, wout_h,
+    n1_ref, qkv_ref, o_ref, lse_ref, orecv, wa, small, y1_ref, n2_ref, c_ref, dyx, win, wout,
+    xall, wq, olow, tb_ref,
+    xs, xr, ws, wr_, os_, or_, ds, dr, fs, fr, ls,
+    *, ndp, nz, hg, hd, scale, experts,
 ):
-    span = x_ref.shape[0]
-    count = span // block
+    d = lax.axis_index("dp")
+    z = lax.axis_index("z")
+    c = lax.axis_index("core")
+    span, model = xall.shape
+    slots = x_ref.shape[1]
+    block = 2 * slots
     width = hg * hd
-    length = len_ref[0]
-    gain = gain_ref[...].astype(F32)
-    for i in range(count):
+    me = z * 2 + c
+    part = wq_l.shape[0]
+    hid = win.shape[2]
+    own = d * 2 + c
+
+    barrier = pltpu.get_barrier_semaphore()
+    count = 0
+    for k in range(ndp):
+        for cc in range(2):
+            if k or cc:
+                pl.semaphore_signal(
+                    barrier, inc=1, device_id_type=MESH,
+                    device_id={"dp": xor(d, k), "z": z, "core": xor(c, cc)},
+                )
+                count += 1
+    for k in range(1, 2 * nz):
+        t = lax.rem(me + k, 2 * nz)
+        tz = lax.div(t, 2)
+
+        @pl.when(tz != z)
+        def greet():
+            pl.semaphore_signal(
+                barrier, inc=1, device_id_type=MESH,
+                device_id={"dp": d, "z": tz, "core": lax.rem(t, 2)},
+            )
+    pl.semaphore_wait(barrier, count + 2 * nz - 2)
+
+    def x_copy(k):
+        t = lax.rem(me + k, 2 * nz)
+        tc = lax.rem(t, 2)
+        rows = pl.ds(pl.multiple_of(me * slots, slots), slots)
+        return remote(x_ref.at[tc], xall.at[rows, :], xs.at[k], xr.at[k], d, lax.div(t, 2), tc)
+
+    for k in range(1, 2 * nz):
+        x_copy(k).start()
+    xall[pl.ds(pl.multiple_of(me * slots, slots), slots), :] = x_ref[c]
+
+    def win_block(index):
+        if len(win_h.shape) == 4:
+            return win_h.at[index]
+        return win_h.at[:, :, pl.ds(pl.multiple_of(index * hid, 128), hid)]
+
+    def w_copy(k, which):
+        peer = xor(d, k)
+        rows = pl.ds(pl.multiple_of(d * part, part), part)
+        if which == 0:
+            pair = (wq_l, wq.at[rows, :])
+        elif which == 1:
+            pair = (wa_l, wa.at[rows, :])
+        elif which == 2:
+            pair = (small_l, small.at[d])
+        else:
+            pair = (win_block(peer * 2 + c), win.at[:, rows, :])
+        return remote(*pair, ws.at[which, k], wr_.at[which, k], peer, z, c)
+
+    for which in (2, 0, 1):
+        for k in range(1, ndp):
+            w_copy(k, which).start()
+    rows_d = pl.ds(pl.multiple_of(d * part, part), part)
+    wq[rows_d, :] = wq_l[...]
+    wa[rows_d, :] = wa_l[...]
+    small[pl.ds(d, 1)] = small_l[...][None]
+    win_own = pltpu.make_async_copy(win_block(own), win.at[:, rows_d, :], ls.at[0])
+    win_own.start()
+    out_rows = pl.ds(pl.multiple_of(c * hid, 16), hid)
+    wout_own = pltpu.make_async_copy(wout_h.at[:, out_rows, :], wout, ls.at[1])
+    wout_own.start()
+    for m in range(2):
+        place = me * slots + lax.broadcasted_iota(jnp.int32, (slots, 1), 0)
+        keep = place < len_ref[m]
+        rows = pl.ds(m * slots, slots)
+        dyx[own, rows, :model] = jnp.where(keep, cot_ref[m].astype(F32), 0.0).astype(BF16)
+    dyx[own, :, model:] = route_ref[...]
+    for head in range(hg):
+        for delta in range(span // block):
+            tb_ref[head, delta] = bias_tile(rd_ref, head, delta, span, block)
+
+    for k in range(1, ndp):
+        w_copy(k, 2).wait_recv()
+        w_copy(k, 0).wait_recv()
+    for k in range(1, ndp):
+        w_copy(k, 3).start()
+
+    def dy_copy(k):
+        return remote(dyx.at[own], dyx.at[own], ds.at[k], dr.at[k], xor(d, k), z, c)
+
+    def dy_pass(k):
+        slot = dyx.at[xor(d, k) * 2 + c]
+        return remote(slot, slot, fs.at[k], fr.at[k], d, z, 1 - c)
+
+    dy_pass(0).start()
+    for k in range(1, ndp):
+        dy_copy(k).start()
+
+    for k in range(1, 2 * nz):
+        x_copy(k).wait_recv()
+    gains = jnp.concatenate([small[i] for i in range(ndp)], axis=1)
+    gain = gains[0:1, :]
+    length = len_ref[c]
+    for i in range(span // block):
         rows = slice(i * block, (i + 1) * block)
-        x = x_ref[rows, :].astype(F32)
+        x = xall[rows, :].astype(F32)
         n1 = (x * rms_scale(x) * gain).astype(BF16)
         n1_ref[rows, :] = n1
-        qkv_ref[rows, :] = dot_nn(n1, w_ref[...]).astype(BF16)
-    for head in range(hg):
-        for delta in range(count):
-            tb_ref[head, delta] = bias_tile(rd_ref, head, delta, span, block)
+        qkv_ref[rows, :] = dot_nn(n1, wq[...]).astype(BF16)
+
+    def o_copy(t):
+        rows = pl.ds(t * slots, slots)
+        return remote(
+            olow.at[rows, :], orecv.at[z, c], os_.at[t], or_.at[me], d, t // 2, t % 2
+        )
+
+    def o_land(t):
+        slot = orecv.at[t // 2, t % 2]
+        return remote(slot, slot, os_.at[t], or_.at[t], d, t // 2, t % 2)
+
     lane = lax.broadcasted_iota(jnp.int32, (block, 128), 1)
-    for i in range(count):
+    for i in range(span // block):
         rows = slice(i * block, (i + 1) * block)
         lse_all = jnp.zeros((block, 128), F32)
         outs = []
@@ -106,33 +251,109 @@
             lse_all = jnp.where(lane == head, top + jnp.log(total), lse_all)
         out = jnp.concatenate(outs, axis=1)
         o_ref[rows, :] = out
-        olow_ref[rows, :] = out.astype(BF16)
+        olow[rows, :] = out.astype(BF16)
         lse_ref[rows, :] = lse_all
+        for t in (2 * i, 2 * i + 1):
+
+            @pl.when(t != me)
+            def away():
+                o_copy(t).start()
+
+            @pl.when(t == me)
+            def stay():
+                orecv[z, c] = olow[t * slots : (t + 1) * slots, :]
+
+    for k in range(1, ndp):
+        dy_copy(k).wait_recv()
+        dy_pass(k).start()
+        w_copy(k, 1).wait_recv()
+
+    for t in range(2 * nz):
+
+        @pl.when(t != me)
+        def landed():
+            o_land(t).wait_recv()
+
+    gain_two = gains[1:2, :]
+    for m in range(2):
+        rows = slice(m * slots, (m + 1) * slots)
+        y1 = x_ref[m].astype(F32)
+        for g in range(nz):
+            if g * width < model:
+                y1 = y1 + dot_nn(orecv[g, m], wa[g * width : (g + 1) * width, :])
+        n2 = (y1 * rms_scale(y1) * gain_two).astype(BF16)
+        y1_ref[rows, :] = y1
+        n2_ref[rows, :] = n2
+        logits = dot_nt(n2, gains.astype(BF16))[:, 2 : 2 + experts]
+        c_ref[rows, :] = gate_weights(logits, route_ref[rows, :].astype(F32), experts)
+
+    for k in range(1, 2 * nz):
+        x_copy(k).wait_send()
+    for k in range(1, ndp):
+        w_copy(k, 3).wait_recv()
+        dy_pass(k).wait_recv()
+        dy_pass(k).wait_send()
+        dy_copy(k).wait_send()
+        for which in range(4):
+            w_copy(k, which).wait_send()
+    dy_pass(0).wait()
+    win_own.wait()
+    wout_own.wait()
+    for t in range(2 * nz):
+
+        @pl.when(t != me)
+        def sent():
+            o_copy(t).wait_send()
+
+
+def front(length, x, cot, route, rd, wq_l, wa_l, small_l, win_h, wout_h, ndp, nz, hg, hd, scale, experts, heads):
+    slots, model = x.shape[1:]
+    span = nz * 2 * slots
+    width = hg * hd
+    rows = 2 * slots
+    hid = wout_h.shape[1] // 2
+    any_spec = pl.BlockSpec(memory_space=pl.ANY)
+    dma = pltpu.SemaphoreType.DMA
+    shape = jax.ShapeDtypeStruct
+    return pl.pallas_call(
+        functools.partial(front_kernel, ndp=ndp, nz=nz, hg=hg, hd=hd, scale=scale, experts=experts),
+        out_shape=(
+            shape((span, model), BF16),
+            shape((span, 3 * width), BF16),
+            shape((span, width), F32),
+            shape((span, 128), F32),
+            shape((nz, 2, slots, width), BF16),
+            shape((nz * width, model), BF16),
+            shape((ndp,) + small_l.shape, F32),
+            shape((rows, model), F32),
+            shape((rows, model), BF16),
+            shape((rows, experts), F32),
+            shape((ndp * 2, rows, model + 128), BF16),
+            shape((experts, model, hid), BF16),
+            shape((experts, hid, model), BF16),
+        ),
+        in_specs=[pl.BlockSpec(memory_space=pltpu.SMEM)] + vmem_specs(7) + [any_spec] * 2,
+        out_specs=tuple(vmem_specs(13)),
+        scratch_shapes=[
+            pltpu.VMEM((span, model), BF16),
+            pltpu.VMEM((model, 3 * width), BF16),
+            pltpu.VMEM((span, width), BF16),
+            pltpu.VMEM((hg, span // rows, rows, rows), F32),
+            dma((2 * nz,)), dma((2 * nz,)),
+            dma((4, ndp)), dma((4, ndp)),
+            dma((2 * nz,)), dma((2 * nz,)),
+            dma((ndp,)), dma((ndp,)), dma((ndp,)), dma((ndp,)),
+            dma((2,)),
+        ],
+        compiler_params=pltpu.CompilerParams(
+            vmem_limit_bytes=VMEM_LIMIT, collective_id=0, has_side_effects=True
+        ),
+        name="front",
+    )(length, x, cot, route, rd, wq_l, wa_l, small_l, win_h, wout_h)
 
 
 def vmem_specs(count):
     return [pl.BlockSpec(memory_space=pltpu.VMEM)] * count
-
-
-def attend(length, x_all, gain, w, rd, hg, hd, scale):
-    span, model = x_all.shape
-    block = 256
-    width = hg * hd
-    return pl.pallas_call(
-        functools.partial(attend_kernel, hg=hg, hd=hd, block=block, scale=scale),
-        out_shape=(
-            jax.ShapeDtypeStruct((span, model), BF16),
-            jax.ShapeDtypeStruct((span, 3 * width), BF16),
-            jax.ShapeDtypeStruct((span, width), F32),
-            jax.ShapeDtypeStruct((span, width), BF16),
-            jax.ShapeDtypeStruct((span, 128), F32),
-        ),
-        in_specs=[pl.BlockSpec(memory_space=pltpu.SMEM)] + vmem_specs(4),
-        out_specs=tuple(vmem_specs(5)),
-        scratch_shapes=[pltpu.VMEM((hg, span // block, block, block), F32)],
-        compiler_params=pltpu.CompilerParams(vmem_limit_bytes=VMEM_LIMIT),
-        name="attend",
-    )(length, x_all, gain, w, rd)
 
 
 def skew_sum(tile):
@@ -320,58 +541,52 @@
     z = lax.axis_index("z")
     core = lax.axis_index("core")
     x_loc = tokens[:, 0]
-    query_pos = (z * 2 + core) * slots + jnp.arange(slots, dtype=jnp.int32)
-    valid = query_pos[None, :] < lengths
-    dy_loc = jnp.where(valid[:, :, None], cotangent[:, 0], 0).reshape(micro * slots, model)
-
-    x_all = lax.all_to_all(x_loc, "core", 0, 1, tiled=True)[0]
-    x_all = lax.all_gather(x_all, "z", axis=0, tiled=True)
     wq = w_qkv.reshape(-1, 3, heads, hd)
     wq = jnp.pad(wq, ((0, 0), (0, 0), (0, pad_heads), (0, 0)))
     wq = lax.dynamic_slice_in_dim(wq, z * hg, hg, 2).reshape(-1, 3 * width)
-    wq = lax.all_gather(wq, "dp", axis=0, tiled=True)
-    wa = lax.all_gather(w_attn, "dp", axis=0, tiled=True)
-    wr = lax.all_gather(w_router, "dp", axis=0, tiled=True)
-    ga = lax.all_gather(gain_attn, "dp", axis=0, tiled=True)
-    gm = lax.all_gather(gain_moe, "dp", axis=0, tiled=True)
     share = ff // (ndp * nz * 2)
     hidden_count = nz * share
-    win = w_expert_in.reshape(experts, -1, ndp, nz, 2, share)
-    win = lax.dynamic_index_in_dim(win, core, 4, keepdims=False)
-    win = win.transpose(2, 1, 0, 3, 4).reshape(ndp, -1, experts * hidden_count)
-    win = lax.all_to_all(win, "dp", 0, 0, tiled=True).reshape(model, experts * hidden_count)
-    wout = w_expert_out.reshape(experts, nz, 2, share, model)
-    wout = lax.dynamic_index_in_dim(wout, core, 2, keepdims=False)
-    wout = wout.reshape(experts * hidden_count, model)
-    dy = lax.all_gather(dy_loc, PLANE, axis=0, tiled=True)
+    small = jnp.concatenate([gain_attn[None], gain_moe[None], w_router.T], axis=0).astype(F32)
+    small = jnp.pad(small, ((0, 8 - small.shape[0]), (0, 0)))
+    route = jnp.pad(routes.reshape(micro * slots, 2).astype(BF16), ((0, 0), (0, 126)))
 
     turned = rel_table[::-1]
     onehot = (turned[:, None] == jnp.arange(buckets_count, dtype=jnp.int32)[None, :]).astype(F32)
     bias_rows = jnp.pad(rel_bias.T, ((0, pad_heads), (0, 0)))
     bias_rows = lax.dynamic_slice_in_dim(bias_rows, z * hg, hg, 0)
     rd = lax.dot_general(bias_rows, onehot, (((1,), (1,)), ((), ())), precision=HIGH)
-    rd = jnp.pad(rd, ((0, 0), (0, 256)))
+    rd = jnp.pad(rd, ((0, 0), (0, 2 * slots)))
     length = lax.dynamic_index_in_dim(lengths[:, 0], core, 0, keepdims=True)
 
-    n1, qkv, o, olow, lse = attend(length, x_all, ga[None, :], wq, rd, hg, hd, scale)
-    olow = olow.reshape(nz * 2, slots, width)
-    olow = lax.all_to_all(olow, COLUMN, 0, 0, tiled=True)
-    olow = olow.reshape(nz, 2, slots, width).transpose(1, 2, 0, 3)
-    olow = olow.reshape(micro * slots, nz * width)[:, :model]
-
+    w_in = w_expert_in
+    if hidden_count % 128:
+        w_in = w_in.reshape(experts, -1, ndp * 2, hidden_count).transpose(2, 0, 1, 3)
+    n1, qkv, o, lse, orecv, wa, small, y1, n2, c, dyx, win, wout = front(
+        lengths[:, 0], x_loc, cotangent[:, 0], route, rd, wq, w_attn, small,
+        w_in, w_expert_out, ndp, nz, hg, hd, scale, experts, heads,
+    )
+    olow = orecv.transpose(1, 2, 0, 3).reshape(micro * slots, nz * width)[:, :model]
+    gains = small.transpose(1, 0, 2).reshape(8, model)
+    ga = gains[0]
+    gm = gains[1]
+    wr = gains[2 : 2 + experts].astype(BF16).T
+    wa = wa[:model]
     x = x_loc.reshape(micro * slots, model).astype(F32)
-    y1 = x + dot_nn(olow, wa)
+    own = lax.axis_index("dp") * 2 + core
+    dy = dyx[:, :, :model].reshape(-1, model)
+    dy_loc = lax.dynamic_index_in_dim(dyx, own, 0, keepdims=False)[:, :model]
+    wq = lax.all_gather(wq, "dp", axis=0, tiled=True)
+    win = win.transpose(1, 0, 2).reshape(model, experts * hidden_count)
+    wout = wout.reshape(experts * hidden_count, model)
     r2 = rms_scale(y1)
     z2 = y1 * r2
-    gain_two = gm.astype(F32)
-    n2 = (z2 * gain_two).astype(BF16)
+    gain_two = gm
     logits = dot_nn(n2, wr)
     chosen = (
         routes.reshape(micro * slots, 2)[:, :, None] == jnp.arange(experts)[None, None, :]
     ).astype(F32)
     routed = jnp.sum(chosen * logits[:, None, :], axis=-1)
     gates = jax.nn.softmax(routed, axis=-1)
-    c = jnp.sum(chosen * gates[:, :, None], axis=1)
 
     n2_all = lax.all_gather(n2, PLANE, axis=0, tiled=True)
     c_all = lax.all_gather(c, PLANE, axis=0, tiled=True)
@@ -401,18 +616,21 @@
     dn1 = lax.all_to_all(dn1, "core", 1, 0, tiled=True).reshape(micro * slots, model).astype(F32)
     r1 = rms_scale(x)
     z1 = x * r1
-    d_norm, g_gain_attn = norm_back(dn1, z1, ga.astype(F32), r1)
+    d_norm, g_gain_attn = norm_back(dn1, z1, ga, r1)
     d_tokens = (dy1 + d_norm).astype(BF16)
 
     piece = model // (ndp * nz * 2)
-    g_out = lax.psum_scatter(
-        dwout.reshape(experts, nz, share, model), "z", scatter_dimension=1, tiled=True
-    ).reshape(experts, share, model).astype(F32)
+    g_out = dwout.reshape(experts, 1, nz // 2, 2, share, model)
+    spread = jnp.zeros((experts, 2, nz // 2, 2, share, model), BF16)
+    g_out = lax.dynamic_update_slice_in_dim(spread, g_out, core, 1)
+    g_out = g_out.reshape(experts, nz * 2, share, model)
+    g_out = lax.psum_scatter(g_out, COLUMN, scatter_dimension=1, tiled=True)
+    g_out = g_out.reshape(experts, share, model).astype(F32)
     g_in = dwin.reshape(ndp, nz, 2, piece, experts * hidden_count)
     g_in = lax.psum_scatter(g_in, "z", scatter_dimension=1, tiled=True)
     g_in = g_in.reshape(ndp * 2, piece, experts * hidden_count)
     g_in = lax.all_to_all(g_in, PLANE, 0, 0, tiled=True)
-    g_in = g_in.reshape(ndp, 2, piece, experts, nz, share).transpose(3, 2, 0, 4, 1, 5)
+    g_in = g_in.reshape(ndp, 2, piece, experts, hidden_count).transpose(3, 2, 0, 1, 4)
     g_in = g_in.reshape(experts, piece, ff).astype(F32)
     g_qkv = g_qkv.reshape(ndp, nz, 2, piece, 3 * width).transpose(0, 2, 1, 3, 4)
     g_qkv = g_qkv.reshape(ndp * 2, nz, piece, 3 * width)

time: 768 us -> 677 us (0.88)
  Pallas kernels: 81.9 us -> 158 us
  blocking collectives: 148 us -> 74.1 us
  waiting for transfers between devices: 396 us -> 355 us
  local copies, waits for them, and re-layouts: 74.9 us -> 36.5 us
    pallas_call x1, Pallas kernels: 10.6 us -> 86.3 us  [front(): pl.pallas_call(functools.partial(front_kernel, ndp=ndp, nz=nz, hg=hg, hd=...]
    all_gather x1 -> x0, blocking collectives: 36.6 us -> none  [local(): wr = lax.all_gather(w_router, 'dp', axis=0, tiled=True)]
    all_to_all x2 -> x0, blocking collectives: 33.2 us -> none  [the longest x1 27.2 us: local(): do = lax.all_to_all(do, COLUMN, 0, 0, tiled=True).reshape(span, width)]
    reshape x4 -> x2, local copies, waits for them, and re-layouts: 27.7 us -> 1.8 us  [the longest x1 1.72 us: local(): win = win.transpose(1, 0, 2).reshape(model, experts * hidden_count)]
    reduce_scatter x1, waiting for transfers between devices: 23.6 us -> 2.83 us  [local(): g_out = lax.psum_scatter(g_out, COLUMN, scatter_dimension=1, tiled=True)]
    reduce_scatter x1, waiting for transfers between devices: 36.1 us -> 17.9 us  [local(): g_qkv = lax.psum_scatter(g_qkv, PLANE, scatter_dimension=0, tiled=True)[0]]
    all_gather x1, waiting for transfers between devices: 0.01 us -> 13.6 us  [local(): n2_all = lax.all_gather(n2, PLANE, axis=0, tiled=True)]
    dynamic_slice x3 -> x0, local copies, waits for them, and re-layouts: 13.1 us -> none  [the longest x2 9.83 us: local(): win = lax.dynamic_index_in_dim(win, core, 4, keepdims=False)]
  transfers between devices with their start and end apart: 16 -> 12, of which waited for: 11 -> 11; matrix products, arithmetic and copies ran while one was open for 11% -> 7% of each run, Pallas kernels for 4% -> 3%
where the time goes in v2:
time: 677 us; the launch traced here: 668 us
  waiting for transfers between devices  355 us (52%)
  Pallas kernels  158 us (23%)
  blocking collectives  74.1 us (11%)
  local copies, waits for them, and re-layouts  36.5 us (5%)
  between operations  14.7 us (2%)
  starting transfers between devices  13.2 us (2%)
  other arithmetic  11.9 us (2%)
    reduce_scatter x1, waiting for transfers between devices, local(): lax.psum_scatter(g_attn, EVERY, scatter_dimension=0, tiled=True).astype(F32)  97.1 us
    pallas_call x1, Pallas kernels, front(): pl.pallas_call(functools.partial(front_kernel, ndp=ndp, nz=nz, hg=hg, hd=...  86.3 us
    pallas_call x1, Pallas kernels, expert_layer(): pl.pallas_call(functools.partial(expert_kernel, experts=experts, hidden_c...  50.5 us
    reduce_scatter x1, waiting for transfers between devices, local(): lax.psum_scatter(dn2_part, PLANE, scatter_dimension=0, tiled=True)  48.5 us
    reduce_scatter x1, waiting for transfers between devices, local(): y = lax.psum_scatter(y_part, PLANE, scatter_dimension=0, tiled=True)  48.4 us
    unnamed x10, waiting for transfers between devices  44.9 us
    psum x1, blocking collectives, local(): small = lax.psum(small, EVERY)  41.3 us
    reduce_scatter x1, waiting for transfers between devices, local(): dn1 = lax.psum_scatter(dn1, 'z', scatter_dimension=0, tiled=True)[0]  34.1 us
  transfers between devices with their start and end apart: 12, of which 11 were waited for; matrix products, arithmetic and copies ran while one was open for 7% of the time, Pallas kernels for 3%

profile of v2, /device:TPU:0, one launch (start us, length us, event | category | flops | bytes accessed | tf_op | source)
XLA Modules:
  0.0 668.4 jit_solution(383774512517650925)
XLA Ops:
  13.0 86.3 %front.1 = (bf16[1024,768]{1,0:T(8,128)(2,1)}, bf16[1024,576]{1,0:T(8,128)(2,1)}, f32[1024,192]{1,0:T(8,128)}, f32[1024,128]{1,0:T(8,128)}, bf16[4,2,128,192]{3,...) custom-call(s32[2]{0:T(128)} %bitcast.125, ...), custom_call_target="tpu_custom_call" | custom-call | tf_op jit(solution)/shard_map/front/pallas_call | solution.py:318
  99.4 3.9 slice.22
  103.3 1.7 copy.143
  105.0 13.7 %all_gather.10.c_ref = f32[2048,4]{1,0:T(8,128)} all-gather(f32[256,4]{1,0:T(8,128)S(1)} %copy-done.10), channel_id=1, replica_groups=mesh['dp'=4,'z'=4,'core'=2] {'dp','core'}, dimensions={0}, use_global_device_ids=true | all-gather | bytes 36864 | tf_op jit(solution)/shard_map/all_gather | solution.py:592
  118.7 13.6 %all-gather.2.cloned.1.call-done.n2_ref = bf16[2048,768]{1,0:T(8,128)(2,1)} async-done(((bf16[256,768]{1,0:T(8,128)(2,1)}), bf16[2048,768]{1,0:T(8,128)(2,1)}) %all-gather.2.cloned.1.call-update) | async-done | bytes 3145744 | tf_op jit(solution)/shard_map/all_gather | solution.py:591
  132.3 50.5 %experts.1 = (bf16[2048,768]{1,0:T(8,128)(2,1)}, bf16[2048,768]{1,0:T(8,128)(2,1)}, f32[2048,4]{1,0:T(8,128)}, bf16[768,1536]{1,0:T(8,128)(2,1)}, bf16[1536,768]{1,0:T(8,128)(2,1)}) custom-call(bf16[2048,768]{1,0:T(8,128)(2,1)} %all-gather.2.cloned.1.call-done.n2_ref, bf16[2048,768]{1,0:T(8,128)(2,1)} %bitcast.94, f32[2048,4]{1,0:T(8,128)} %all_gather.10.c_ref, ...), custom_call_target="tpu_custom_call" | custom-call | tf_op jit(solution)/shard_map/experts/pallas_call | solution.py:509
  186.2 32.9 %reduce-scatter.15.cloned.1.call-done = f32[256,4]{1,0:T(8,128)} async-done(((f32[2048,4]{1,0:T(8,128)}), f32[256,4]{1,0:T(8,128)}) %reduce-scatter.15.cloned.1.call-update) | async-done | bytes 4112 | tf_op jit(solution)/shard_map/reduce_scatter | solution.py:596
  220.2 48.5 %reduce-scatter.13.cloned.1.call-done = bf16[256,768]{1,0:T(8,128)(2,1)} async-done(((bf16[2048,768]{1,0:T(8,128)(2,1)}), bf16[256,768]{1,0:T(8,128)(2,1)}) %reduce-scatter.13.cloned.1.call-update) | async-done | bytes 393232 | tf_op jit(solution)/shard_map/reduce_scatter | solution.py:595
  270.2 48.4 %reduce-scatter.11.cloned.1.call-done = bf16[256,768]{1,0:T(8,128)(2,1)} async-done(((bf16[2048,768]{1,0:T(8,128)(2,1)}), bf16[256,768]{1,0:T(8,128)(2,1)}) %reduce-scatter.11.cloned.1.call-update) | async-done | bytes 393232 | tf_op jit(solution)/shard_map/reduce_scatter | solution.py:594
  318.6 2.1 multiply_add_fusion
  322.3 4.6 all-to-all-start
  327.6 15.0 %all_gather.11.w_ref = bf16[768,576]{1,0:T(8,128)(2,1)} all-gather(bf16[192,576]{1,0:T(8,128)(2,1)S(1)} %copy-done.7), channel_id=1, replica_groups=mesh['dp'=4,'z'=4,'core'=2] {'dp'}, dimensions={0}, use_global_device_ids=true | all-gather | bytes 1105920 | tf_op jit(solution)/shard_map/all_gather | solution.py:578
  342.6 6.7 %all-to-all-done = bf16[8,128,192]{1,2,0:T(8,128)(2,1)S(1)} async-done(((bf16[8,128,192]{1,2,0:T(8,128)(2,1)}), bf16[8,128,192]{1,2,0:T(8,128)(2,1)S(1)}, u32[]{:S(2)}, u32[]{:S(2)}) %all-to-all-start) | async-done | bytes 393248 | tf_op jit(solution)/shard_map/all_to_all | solution.py:611
  350.4 20.7 %attend_back.1 = (bf16[1024,768]{1,0:T(8,128)(2,1)}, bf16[768,576]{1,0:T(8,128)(2,1)}, f32[3,1280]{1,0:T(4,128)}) custom-call(s32[1]{0:T(128)} %bitcast.15.len_ref, bf16[1024,768]{1,0:T(8,128)(2,1)} %get-tuple-element.41.n1_ref, bf16[1024,576]{1,0:T(8,128)(2,1)} %get-tuple-element.42.qkv_ref, f32[1024,192]{1,0:T(8,128)} %get-tuple-element.43.o_ref, ...), custom_call_target="tpu_custom_call" | custom-call | tf_op jit(solution)/shard_map/attend_back/pallas_call | solution.py:427
  371.1 2.3 copy.129
  376.2 2.7 broadcast_in_dim.11
  378.9 1.6 copy_dynamic-update-slice_fusion
  381.7 42.9 %all-reduce.6.cloned.1.call-done = bf16[4,4,2,24,1536]{4,3,2,1,0:T(8,128)(2,1)} async-done(((bf16[4,4,2,24,1536]{4,3,2,1,0:T(8,128)(2,1)}), bf16[4,4,2,24,1536]{4,3,2,1,0:T(8,128)(2,1)}) %all-reduce.6.cloned.1.call-update) | async-done | bytes 2359312
  424.6 2.6 constant_dynamic-slice_fusion.2
  427.1 3.7 all-to-all-start.3
  432.7 8.5 %all-to-all-done.3 = bf16[8,24,1536]{2,1,0:T(8,128)(2,1)S(1)} async-done(((bf16[8,24,1536]{2,1,0:T(8,128)(2,1)}), bf16[8,24,1536]{2,1,0:T(8,128)(2,1)S(1)}, u32[]{:S(2)}, u32[]{:S(2)}) %all-to-all-start.3) | async-done | bytes 589856 | tf_op jit(solution)/shard_map/all_to_all | solution.py:632
  442.5 2.0 reshape.298
  444.5 17.9 %reduce-scatter.19.cloned.1.call-done = bf16[1,4,24,576]{3,2,1,0:T(8,128)(2,1)} async-done(((bf16[8,4,24,576]{3,2,1,0:T(8,128)(2,1)}), bf16[1,4,24,576]{3,2,1,0:T(8,128)(2,1)}) %reduce-scatter.19.cloned.1.call-update) | async-done | bytes 110608 | tf_op jit(solution)/shard_map/reduce_scatter | solution.py:637
  462.4 4.6 all-to-all-start.2
  468.0 97.1 %reduce-scatter.21.cloned.1.call-done = bf16[24,768]{1,0:T(8,128)(2,1)} async-done(((bf16[768,768]{1,0:T(8,128)(2,1)}), bf16[24,768]{1,0:T(8,128)(2,1)}) %reduce-scatter.21.cloned.1.call-update) | async-done | bytes 36880 | tf_op jit(solution)/shard_map/reduce_scatter | solution.py:641
  567.8 34.1 %reduce-scatter.17.cloned.1.call-done = bf16[1,1,256,768]{3,2,1,0:T(8,128)(2,1)} async-done(((bf16[4,1,256,768]{3,2,1,0:T(8,128)(2,1)}), bf16[1,1,256,768]{3,2,1,0:T(8,128)(2,1)}) %reduce-scatter.17.cloned.1.call-update) | async-done | bytes 393232 | tf_op jit(solution)/shard_map/reduce_scatter | solution.py:615
  601.9 1.6 copy.154
  604.0 3.1 reduce.10
  607.2 4.0 all_to_all.24
  612.1 41.3 %psum.7 = f32[4992]{0:T(1024)S(1)} all-reduce(f32[4992]{0:T(1024)S(1)} %pad_maximum_fusion), channel_id=1, replica_groups=mesh['dp'=4,'z'=4,'core'=2] {'dp','z','core'}, use_global_device_ids=true, to_apply=%region_18.19 | all-reduce | flops 4992 | bytes 39936 | tf_op jit(solution)/shard_map/psum | solution.py:648
  656.5 2.8 reduce-scatter.23.cloned.1.call-done
  659.3 2.2 bitcast_convert_fusion
  (132 shorter events, 30.1 us)
Async XLA Ops:
  7.2 3.5 copy-start
  7.2 3.3 copy-start.16
  7.2 3.4 copy-start.20
  7.2 3.4 copy-start.21
  7.2 5.2 copy-start.17
  7.2 125.1 %all-gather.2.cloned.1.call-start = ((), (), s32[]{:S(2)}) async-start(), calls=%async_computation.11 | async-start | bytes 3538944 | tf_op jit(solution)/shard_map/all_gather | solution.py:591
  8.0 91.2 %copy-start.14 = (s32[1024]{0:T(1024)}, s32[1024]{0:T(1024)S(1)}, u32[]{:S(2)}) copy-start(s32[1024]{0:T(1024)S(1)} %rev.3) | copy-start | bytes 12292
  99.3 119.8 %reduce-scatter.15.cloned.1.call-start = ((), (), s32[]{:S(2)}) async-start(), calls=%async_computation.14 | async-start | bytes 1179648 | tf_op jit(solution)/shard_map/reduce_scatter | solution.py:596
  99.4 3.9 copy-start.6
  182.9 85.8 %reduce-scatter.13.cloned.1.call-start = ((), (), s32[]{:S(2)}) async-start(), calls=%async_computation.13 | async-start | bytes 3538944 | tf_op jit(solution)/shard_map/reduce_scatter | solution.py:595
  183.6 2.1 copy-start.2
  183.6 135.0 %reduce-scatter.11.cloned.1.call-start = ((), (), s32[]{:S(2)}) async-start(), calls=%async_computation.12 | async-start | bytes 3538944 | tf_op jit(solution)/shard_map/reduce_scatter | solution.py:594
  183.7 2.2 copy-start.4
  184.2 240.3 %all-reduce.6.cloned.1.call-start = ((), (), s32[]{:S(2)}) async-start(), calls=%async_computation.19 | async-start | bytes 4718592
  318.6 2.1 copy-start.8
  320.7 6.3 copy-start.18
  320.7 6.9 %copy-start.7 = (bf16[192,576]{1,0:T(8,128)(2,1)S(1)}, bf16[192,576]{1,0:T(8,128)(2,1)}, u32[]{:S(2)}) copy-start(bf16[192,576]{1,0:T(8,128)(2,1)} %copy.117.wq_l) | copy-start | bytes 663556
  322.3 27.0 %all-to-all-start = ((bf16[8,128,192]{1,2,0:T(8,128)(2,1)}), bf16[8,128,192]{1,2,0:T(8,128)(2,1)S(1)}, u32[]{:S(2)}, u32[]{:S(2)}) async-start(bf16[8,128,192]{1,2,0:T(8,128)(2,1)} %bitcast.17), calls=%async_computation.3 | async-start | bytes 786432 | tf_op jit(solution)/shard_map/all_to_all | solution.py:611
  326.9 135.5 %reduce-scatter.19.cloned.1.call-start = ((), (), s32[]{:S(2)}) async-start(), calls=%async_computation.16 | async-start | bytes 1105920 | tf_op jit(solution)/shard_map/reduce_scatter | solution.py:637
  371.1 2.4 copy-start.9
  373.4 191.7 %reduce-scatter.21.cloned.1.call-start = ((), (), s32[]{:S(2)}) async-start(), calls=%async_computation.17 | async-start | bytes 1216512 | tf_op jit(solution)/shard_map/reduce_scatter | solution.py:641
  375.4 226.4 %reduce-scatter.17.cloned.1.call-start = ((), (), s32[]{:S(2)}) async-start(), calls=%async_computation.15 | async-start | bytes 1966080 | tf_op jit(solution)/shard_map/reduce_scatter | solution.py:615
  376.2 283.1 %reduce-scatter.23.cloned.1.call-start = ((), (), s32[]{:S(2)}) async-start(), calls=%async_computation.18 | async-start | bytes 5308416 | tf_op jit(solution)/shard_map/reduce_scatter | solution.py:627
  376.2 2.7 copy-start.5
  380.5 50.3 %copy-start.3 = (bf16[2,1,128,768]{3,2,1,0:T(8,128)(2,1)S(1)}, bf16[2,1,128,768]{3,2,1,0:T(8,128)(2,1)}, u32[]{:S(2)}) copy-start(bf16[2,1,128,768]{3,2,1,0:T(8,128)(2,1)} %param.13) | copy-start | bytes 1179652
  427.1 14.1 %all-to-all-start.3 = ((bf16[8,24,1536]{2,1,0:T(8,128)(2,1)}), bf16[8,24,1536]{2,1,0:T(8,128)(2,1)S(1)}, u32[]{:S(2)}, u32[]{:S(2)}) async-start(bf16[8,24,1536]{2,1,0:T(8,128)(2,1)} %bitcast.34), calls=%async_computation.9 | async-start | bytes 1179648 | tf_op jit(solution)/shard_map/all_to_all | solution.py:632
  441.6 25.4 %copy-start.15 = (s32[1024]{0:T(1024)S(1)}, s32[1024]{0:T(1024)}, u32[]{:S(2)}) copy-start(s32[1024]{0:T(1024)} %copy-done.14) | copy-start | bytes 12292
  442.5 24.5 %copy-start.19 = (f32[3,1280]{1,0:T(4,128)S(1)}, f32[3,1280]{1,0:T(4,128)}, u32[]{:S(2)}) copy-start(f32[3,1280]{1,0:T(4,128)} %get-tuple-element.49) | copy-start | bytes 46084
  462.4 104.1 %all-to-all-start.2 = ((bf16[4,24,576]{2,1,0:T(8,128)(2,1)}), bf16[4,24,576]{2,1,0:T(8,128)(2,1)S(1)}, u32[]{:S(2)}, u32[]{:S(2)}) async-start(bf16[4,24,576]{2,1,0:T(8,128)(2,1)} %bitcast.121), calls=%async_computation.7 | async-start | bytes 245760 | tf_op jit(solution)/shard_map/all_to_all | solution.py:638
  601.9 9.8 %copy-start.12 = (f32[256]{0:T(256)S(1)}, f32[256]{0:T(256)}, u32[]{:S(2)}) copy-start(f32[256]{0:T(256)} %rsqrt_bitcast_fusion) | copy-start | bytes 3076
  604.0 8.1 %copy-start.11 = (f32[3072]{0:T(1024)S(1)}, f32[3072]{0:T(1024)}, u32[]{:S(2)}) copy-start(f32[3072]{0:T(1024)} %reshape.287) | copy-start | bytes 36868
  611.7 49.8 %copy-start.1 = (f32[32,12]{0,1:T(8,128)S(1)}, f32[32,12]{0,1:T(8,128)}, u32[]{:S(2)}) copy-start(f32[32,12]{0,1:T(8,128)} %param.17) | copy-start | bytes 4612
  (3 other events, 3.1 us)
Sparse Core Ops, SparseCore 0:
  99.4 32.8 all-gather.1
  183.0 36.0 reduce-scatter.14
  222.5 46.1 reduce-scatter.12
  272.3 46.2 reduce-scatter.10
  320.8 103.7 all-reduce.5
  427.6 34.7 reduce-scatter.18
  468.9 96.1 reduce-scatter.20
  567.5 34.3 reduce-scatter.16
  604.3 54.9 reduce-scatter.22
